TPU v7x, 32 devices: a whole 2x2x4 slice. The times are simulated.
32 devices in a mesh: members: 2 (over x), lon: 16 (over z, y, core).
Axes of the slice: x: 2, y: 2, z: 4, core: 2. Of those that a mesh axis runs over, the one named last changes fastest.
Arguments:
- state: bfloat16 [262144, 128], P(('members', 'lon')), parts along dimension 0, may hold values from -6 to 6
- cotangent: bfloat16 [262144, 128], P(('members', 'lon')), parts along dimension 0, may hold values from -6 to 6
- local_interp: bfloat16 [2048, 128, 128], P(('members', 'lon')), parts along dimension 0, may hold values from -0.5 to 0.5
- remote_interp: bfloat16 [384, 128, 128], P(('members', 'lon')), parts along dimension 0, may hold values from -0.5 to 0.5
- departures: int32 [3, 384], P(None, ('members', 'lon')), parts along dimension 1, may hold values from 0 to 63, as said below
- counts: int32 [32], P(('members', 'lon')), parts along dimension 0, may hold values from 3 to 12, as said below
- w_in: bfloat16 [128, 256], replicated, may hold values from -0.5 to 0.5
- b_in: float32 [256], replicated, may hold values from -4 to 4
- w_out: bfloat16 [256, 128], replicated, may hold values from -0.375 to 0.375
Outputs:
- grad_state: bfloat16 [262144, 128], P(('members', 'lon')), parts along dimension 0
- grad_w_in: float32 [256, 256], P('members'), parts along dimension 0
- grad_b_in: float32 [512], P('members'), parts along dimension 0
- grad_w_out: float32 [512, 128], P('members'), parts along dimension 0
There are 2 independent parts, one for each index of `members`. A program takes and returns all parts, laid end to end along the dimension named above; an argument that names none is the same for every part. Nothing has to cross between parts.
Inputs may be any that keep to these rules, and one draw needn't show every extreme that they name: `departures`: A live entry's source tile lies within 3 sectors of its own tile, cyclically in longitude. Among the live entries of one tile at most 2 name one source tile, and every draw has a tile where that most is reached. Blocks are block numbers within a tile. `counts`: some tile uses all 12 entries.
All inputs are finite; a program needn't handle non-finite values.
Results may differ from a plain program's by a relative error of at most 0.0068.
Values may be sent and summed in bfloat16 or wider, within the bound.
A program may use at most 64 MiB of HBM per device.

v0:
```python
import jax
import jax.numpy as jnp
from jax import lax
from jax.sharding import PartitionSpec as P

CAP = 2
REACH = 3


def from_behind(array, axis, by):
    count = lax.axis_size(axis)
    return lax.ppermute(array, axis, [(i, (i + by) % count) for i in range(count)])


def rank_slots(sources, alive):
    count = sources.shape[0]
    order = jnp.arange(count, dtype=jnp.int32)
    earlier = (
        (sources[:, None] == sources[None, :]) & alive[None, :] & (order[None, :] < order[:, None])
    )
    return jnp.sum(earlier.astype(jnp.int32), axis=1)


def body(state, cotangent, local_interp, remote_interp, departures, counts, w_in, b_in, w_out):
    nblocks = local_interp.shape[0]
    width = local_interp.shape[1]
    feat = state.shape[1]
    entries = remote_interp.shape[0]
    tiles = lax.axis_size("lon")
    myself = lax.axis_index("lon")
    blocks = state.reshape(nblocks, width, feat)
    sources = departures[0]
    source_blocks = departures[1]
    targets = departures[2]
    alive = jnp.arange(entries, dtype=jnp.int32) < counts[0]
    ahead = (sources - myself + tiles) % tiles
    signed = jnp.where(ahead > tiles // 2, ahead - tiles, ahead)
    slots = rank_slots(sources, alive)
    span = 2 * REACH + 1
    spots = jnp.where(alive, (signed + REACH) * CAP + slots, span * CAP)
    wanted = (
        jnp.full((span * CAP,), -1, jnp.int32)
        .at[spots]
        .set(source_blocks, mode="drop")
        .reshape(span, CAP)
    )
    asked_rows = []
    got_rows = []
    for step in range(span):
        offset = step - REACH
        if offset == 0:
            asked_here = wanted[step]
        else:
            asked_here = from_behind(wanted[step], "lon", offset)
        outgoing = jnp.take(blocks, jnp.clip(asked_here, 0, nblocks - 1), axis=0)
        if offset == 0:
            arrived = outgoing
        else:
            arrived = from_behind(outgoing, "lon", -offset)
        asked_rows.append(asked_here)
        got_rows.append(arrived)
    asked = jnp.stack(asked_rows)
    fetched = jnp.stack(got_rows).reshape(span * CAP, width, feat)
    picked = jnp.take(fetched, jnp.clip(spots, 0, span * CAP - 1), axis=0)
    weight = alive.astype(jnp.float32)[:, None, None]
    contrib = (
        jnp.einsum("ecd,edf->ecf", remote_interp, picked, preferred_element_type=jnp.float32)
        * weight
    )
    yfull = jnp.einsum("tcd,tdf->tcf", local_interp, blocks, preferred_element_type=jnp.float32)
    where_to = jnp.where(alive, targets, nblocks)
    yfull = yfull.at[where_to].add(contrib, mode="drop")
    y_b = yfull.astype(jnp.bfloat16).reshape(nblocks * width, feat)
    pre = jnp.dot(y_b, w_in, preferred_element_type=jnp.float32) + b_in
    hidden = jnp.tanh(pre)
    h_b = hidden.astype(jnp.bfloat16)
    ghid = jnp.einsum("rf,hf->rh", cotangent, w_out, preferred_element_type=jnp.float32)
    gpre = ghid * (1.0 - hidden * hidden)
    gpre_b = gpre.astype(jnp.bfloat16)
    gyfull = cotangent.astype(jnp.float32) + jnp.einsum(
        "rh,fh->rf", gpre_b, w_in, preferred_element_type=jnp.float32
    )
    gy_b = gyfull.astype(jnp.bfloat16).reshape(nblocks, width, feat)
    d_in = jnp.einsum("rf,rh->fh", y_b, gpre_b, preferred_element_type=jnp.float32)
    d_b = jnp.sum(gpre, axis=0)
    d_out = jnp.einsum("rh,rf->hf", h_b, cotangent, preferred_element_type=jnp.float32)
    d_in, d_b, d_out = lax.psum((d_in, d_b, d_out), "lon")
    local_back = jnp.einsum("tdc,tdf->tcf", local_interp, gy_b, preferred_element_type=jnp.float32)
    remote_back = (
        jnp.einsum(
            "edc,edf->ecf",
            remote_interp,
            jnp.take(gy_b, targets, axis=0),
            preferred_element_type=jnp.float32,
        )
        * weight
    )
    outbox = (
        jnp.zeros((span * CAP, width, feat), jnp.float32).at[spots].add(remote_back, mode="drop")
    )
    outbox = outbox.reshape(span, CAP, width, feat)
    total = local_back
    for step in range(span):
        offset = step - REACH
        if offset == 0:
            returned = outbox[step]
        else:
            returned = from_behind(outbox[step], "lon", offset)
        owners_rows = jnp.where(asked[step] >= 0, asked[step], nblocks)
        total = total.at[owners_rows].add(returned, mode="drop")
    grad_state = total.reshape(nblocks * width, feat).astype(jnp.bfloat16)
    return (grad_state, d_in, d_b, d_out)


def solution(mesh):
    return jax.shard_map(
        body,
        mesh=mesh,
        in_specs=(
            P(("members", "lon"), None),
            P(("members", "lon"), None),
            P(("members", "lon"), None, None),
            P(("members", "lon"), None, None),
            P(None, ("members", "lon")),
            P(("members", "lon")),
            P(),
            P(),
            P(),
        ),
        out_specs=(
            P(("members", "lon"), None),
            P("members", None),
            P("members"),
            P("members", None),
        ),
        check_vma=False,
    )
```

profile of v0, /device:TPU:0, one launch (start us, length us, event | category | flops | bytes accessed | tf_op | source)
XLA Modules:
  0.0 187.2 jit_solution(16267246397209711979)
XLA Ops:
  8.0 0.8 slice_bitcast_fusion
  9.0 0.8 fusion.27
  10.5 2.4 %collective-permute-start.10 = (s32[2]{0:T(128)S(1)}, s32[2]{0:T(128)S(1)}, u32[]{:S(2)}, u32[]{:S(2)}) collective-permute-start(s32[2]{0:T(128)S(1)} %get-tuple-element.37), channel_id=1, source_target_pairs={{0,3},{1,4},{2,5},{3,6},{4,7},{5,8},{6,9},{7,10},{8,11},{9,12},{10... | collective-permute-start | bytes 32 | tf_op jit(solution)/shard_map/ppermute | solution.py:12
  12.9 1.5 collective-permute-start.8
  14.8 4.0 %collective-permute-start.4 = (s32[2]{0:T(128)S(1)}, s32[2]{0:T(128)S(1)}, u32[]{:S(2)}, u32[]{:S(2)}) collective-permute-start(s32[2]{0:T(128)S(1)} %get-tuple-element.40), channel_id=1, source_target_pairs={{0,15},{1,0},{2,1},{3,2},{4,3},{5,4},{6,5},{7,6},{8,7},{9,8},{10,9... | collective-permute-start | bytes 32 | tf_op jit(solution)/shard_map/ppermute | solution.py:12
  19.4 0.8 compare_and_fusion.7
  20.8 4.3 %fusion.36 = f32[64,128,128]{2,1,0:T(8,128)} fusion(bf16[64,128,128]{2,1,0:T(8,128)(2,1)} %param.13, bf16[64,128,128]{2,1,0:T(8,128)(2,1)S(1)} %bitcast.74), kind=kOutput, calls=%fused_computation.134 | convolution fusion | flops 268435456 | bytes 8388608 | tf_op jit(solution)/shard_map/tcd,tdf->tcf/dot_general | solution.py:70
  25.5 2.6 %collective-permute-done = s32[2]{0:T(128)S(1)} collective-permute-done((s32[2]{0:T(128)S(1)}, s32[2]{0:T(128)S(1)}, u32[]{:S(2)}, u32[]{:S(2)}) %collective-permute-start) | collective-permute-done | bytes 40 | tf_op jit(solution)/shard_map/ppermute | solution.py:12
  31.6 2.0 %collective-permute-start.11 = (bf16[2,128,128]{2,1,0:T(8,128)(2,1)S(1)}, bf16[2,128,128]{2,1,0:T(8,128)(2,1)S(1)}, u32[]{:S(2)}, u32[]{:S(2)}) collective-permute-start(bf16[2,128,128]{2,1,0:T(8,128)(2,1)S(1)} %broadcast_select_fusion), channel_id=1, source_target_pairs={{0,13},{1,14},{2,15},{3,0},{4,1},{5,2},{6,3},{7,4},{8,5},{9,6},{10... | collective-permute-start | bytes 196616 | tf_op jit(solution)/shard_map/ppermute | solution.py:12
  33.6 2.6 %collective-permute-start.9 = (bf16[2,128,128]{2,1,0:T(8,128)(2,1)S(1)}, bf16[2,128,128]{2,1,0:T(8,128)(2,1)S(1)}, u32[]{:S(2)}, u32[]{:S(2)}) collective-permute-start(bf16[2,128,128]{2,1,0:T(8,128)(2,1)S(1)} %broadcast_select_fusion.1), channel_id=1, source_target_pairs={{0,14},{1,15},{2,0},{3,1},{4,2},{5,3},{6,4},{7,5},{8,6},{9,7},{10,... | collective-permute-start | bytes 196616 | tf_op jit(solution)/shard_map/ppermute | solution.py:12
  37.0 3.6 %collective-permute-start.1 = (bf16[2,128,128]{2,1,0:T(8,128)(2,1)S(1)}, bf16[2,128,128]{2,1,0:T(8,128)(2,1)S(1)}, u32[]{:S(2)}, u32[]{:S(2)}) collective-permute-start(bf16[2,128,128]{2,1,0:T(8,128)(2,1)S(1)} %broadcast_select_fusion.5), channel_id=1, source_target_pairs={{0,3},{1,4},{2,5},{3,6},{4,7},{5,8},{6,9},{7,10},{8,11},{9,12},{10... | collective-permute-start | bytes 196616 | tf_op jit(solution)/shard_map/ppermute | solution.py:12
  42.8 1.6 collective-permute-start.3
  44.5 5.3 %collective-permute-done.3 = bf16[2,128,128]{2,1,0:T(8,128)(2,1)S(1)} collective-permute-done((bf16[2,128,128]{2,1,0:T(8,128)(2,1)S(1)}, bf16[2,128,128]{2,1,0:T(8,128)(2,1)S(1)}, u32[]{:S(2)}, u32[]{:S(2)}) %collective-permute-start.3) | collective-permute-done | bytes 65568 | tf_op jit(solution)/shard_map/ppermute | solution.py:12
  50.0 0.8 copy-done.5
  50.8 1.6 gather_fusion
  52.5 1.4 fusion.8
  53.8 1.4 copy.24
  55.3 3.2 %scatter_fusion = f32[64,128,128]{2,1,0:T(8,128)} fusion(f32[64,128,128]{2,1,0:T(8,128)} %fusion.36, s32[12]{0:T(128)S(1)} %get-tuple-element.35, f32[12,128,128]{2,1,0:T(8,128)S(1)} %copy.24), kind=kCustom, calls=%fused_computation.10 | custom fusion | flops 196608 | bytes 2359344 | tf_op jit(solution)/shard_map/scatter-add | solution.py:72
  58.4 2.6 %convert_element_type.34 = bf16[64,128,128]{2,1,0:T(8,128)(2,1)S(1)} convert(f32[64,128,128]{2,1,0:T(8,128)} %scatter_fusion) | non-fusion elementwise | flops 1048576 | bytes 6291456 | tf_op jit(solution)/shard_map/convert_element_type | solution.py:73
  61.0 1.2 fusion
  62.3 1.0 copy-done.2
  63.4 2.0 %fusion.2 = f32[256,128]{1,0:T(8,128)} fusion(bf16[8192,128]{1,0:T(8,128)(2,1)S(1)} %copy-done.2, f32[8192,256]{1,0:T(8,128)S(1)} %fusion), kind=kOutput, calls=%fused_computation.24 | convolution fusion | flops 538968064 | bytes 10616832 | tf_op jit(solution)/shard_map/rh,rf->hf/dot_general | solution.py:86
  65.3 1.8 fusion.35
  67.2 2.7 %fusion.1 = bf16[8192,128]{1,0:T(8,128)(2,1)} fusion(bf16[128,256]{1,0:T(8,128)(2,1)S(1)} %copy-done.6, bf16[8192,128]{1,0:T(8,128)(2,1)S(1)} %copy-done.2, bf16[8192,256]{1,0:T(8,128)(2,1)S(1)} %get-tuple-element.44), kind=kOutput, calls=%fused_computation.23 | convolution fusion | flops 540016640 | bytes 8454144 | tf_op jit(solution)/shard_map/rh,fh->rf/dot_general | solution.py:80
  69.9 2.9 %gather_fusion.1 = bf16[12,128,128]{2,1,0:T(8,128)(2,1)} fusion(bf16[64,128,128]{2,1,0:T(8,128)(2,1)} %bitcast.84, s32[1024]{0:T(1024)S(1)} %pad_clamp_fusion), kind=kCustom, calls=%fused_computation.8 | custom fusion | bytes 786480 | tf_op jit(solution)/shard_map/jit(_take)/gather | solution.py:93
  72.8 1.4 fusion.7
  74.2 1.2 copy.27
  75.5 2.4 %scatter_fusion.1 = f32[14,128,128]{2,1,0:T(8,128)S(1)} fusion(f32[14,128,128]{2,1,0:T(8,128)S(1)} %broadcast_in_dim.87, s32[12]{0:T(128)S(1)} %fusion.26, f32[12,128,128]{2,1,0:T(8,128)} %copy.27), kind=kCustom, calls=%fused_computation.11 | custom fusion | flops 196608 | bytes 2359344 | tf_op jit(solution)/shard_map/scatter-add | solution.py:99
  77.9 0.8 fusion.34
  78.7 4.4 %fusion.4 = f32[128,256]{1,0:T(8,128)} fusion(bf16[8192,128]{1,0:T(8,128)(2,1)} %bitcast.83, bf16[8192,256]{1,0:T(8,128)(2,1)} %copy-done.1), kind=kOutput, calls=%fused_computation.27 | convolution fusion | flops 536870912 | bytes 6422528 | tf_op jit(solution)/shard_map/rf,rh->fh/dot_general | solution.py:84
  83.1 1.7 collective-permute-start.17
  84.8 0.7 collective-permute-start.15
  85.6 4.0 %collective-permute-start.14 = (f32[2,128,128]{2,1,0:T(8,128)S(1)}, f32[2,128,128]{2,1,0:T(8,128)S(1)}, u32[]{:S(2)}, u32[]{:S(2)}) collective-permute-start(f32[2,128,128]{2,1,0:T(8,128)S(1)} %copy-done.7), channel_id=1, source_target_pairs={{0,15},{1,0},{2,1},{3,2},{4,3},{5,4},{6,5},{7,6},{8,7},{9,8},{10,9... | collective-permute-start | bytes 393224 | tf_op jit(solution)/shard_map/ppermute | solution.py:12
  89.7 1.7 collective-permute-start.13
  91.3 5.1 %convolution_bitcast_fusion = f32[64,128,128]{1,2,0:T(8,128)} fusion(bf16[64,128,128]{2,1,0:T(8,128)(2,1)} %bitcast.85, bf16[64,128,128]{2,1,0:T(8,128)(2,1)} %param.13), kind=kOutput, calls=%fused_computation.26 | convolution fusion | flops 268435456 | bytes 8388608 | tf_op jit(solution)/shard_map/tdc,tdf->tcf/dot_general | solution.py:88
  96.4 5.6 %copy.28 = f32[64,128,128]{2,1,0:T(8,128)} copy(f32[64,128,128]{1,2,0:T(8,128)} %convolution_bitcast_fusion) | data formatting | bytes 8388608 | tf_op jit(solution)/shard_map/tdc,tdf->tcf/dot_general | solution.py:88
  102.0 30.1 %psum.22 = f32[256]{0:T(256)} all-reduce(f32[256]{0:T(256)S(1)} %get-tuple-element.43), channel_id=1, replica_groups=mesh['members'=2,'lon'=16] {'lon'}, use_global_device_ids=true, to_apply=%region_13.15 | all-reduce | flops 256 | bytes 2048 | tf_op jit(solution)/shard_map/psum | solution.py:87
  132.1 2.2 %scatter_fusion.2 = f32[64,128,128]{2,1,0:T(8,128)} fusion(f32[64,128,128]{2,1,0:T(8,128)} %copy.28, s32[2]{0:T(128)} %compare_select_fusion.21, f32[2,128,128]{2,1,0:T(8,128)S(1)} %collective-permute-done.12), kind=kCustom, calls=%fused_computation.12 | custom fusion | flops 32768 | bytes 393224 | tf_op jit(solution)/shard_map/scatter-add | solution.py:110
  134.3 2.3 %scatter_fusion.3 = f32[64,128,128]{2,1,0:T(8,128)} fusion(f32[64,128,128]{2,1,0:T(8,128)} %scatter_fusion.2, s32[2]{0:T(128)} %compare_select_fusion.17, f32[2,128,128]{2,1,0:T(8,128)} %collective-permute-done.13), kind=kCustom, calls=%fused_computation.13 | custom fusion | flops 32768 | bytes 393224 | tf_op jit(solution)/shard_map/scatter-add | solution.py:110
  136.6 2.2 %scatter_fusion.4 = f32[64,128,128]{2,1,0:T(8,128)} fusion(f32[64,128,128]{2,1,0:T(8,128)} %scatter_fusion.3, s32[2]{0:T(128)} %compare_select_fusion.15, f32[2,128,128]{2,1,0:T(8,128)S(1)} %collective-permute-done.14), kind=kCustom, calls=%fused_computation.14 | custom fusion | flops 32768 | bytes 393224 | tf_op jit(solution)/shard_map/scatter-add | solution.py:110
  138.8 2.1 %scatter_fusion.5 = f32[64,128,128]{2,1,0:T(8,128)} fusion(f32[64,128,128]{2,1,0:T(8,128)} %scatter_fusion.4, s32[2]{0:T(128)S(1)} %get-tuple-element.36, f32[2,128,128]{2,1,0:T(8,128)S(1)} %get-tuple-element.26), kind=kCustom, calls=%fused_computation.15 | custom fusion | flops 32768 | bytes 393224 | tf_op jit(solution)/shard_map/scatter-add | solution.py:110
  140.9 1.6 scatter_fusion.6
  142.6 2.1 %scatter_fusion.7 = f32[64,128,128]{2,1,0:T(8,128)} fusion(f32[64,128,128]{2,1,0:T(8,128)} %scatter_fusion.6, s32[2]{0:T(128)S(1)} %compare_select_fusion.9, f32[2,128,128]{2,1,0:T(8,128)S(1)} %collective-permute-done.16), kind=kCustom, calls=%fused_computation.17 | custom fusion | flops 32768 | bytes 393224 | tf_op jit(solution)/shard_map/scatter-add | solution.py:110
  144.6 1.5 scatter_fusion.8
  146.2 3.9 %convert_element_type.37 = bf16[64,128,128]{2,1,0:T(8,128)(2,1)} convert(f32[64,128,128]{2,1,0:T(8,128)} %scatter_fusion.8) | non-fusion elementwise | flops 1048576 | bytes 6291456 | tf_op jit(solution)/shard_map/convert_element_type | solution.py:111
  150.1 27.1 %all-reduce.3.cloned.1.call-done = (f32[128,256]{1,0:T(8,128)}, f32[256,128]{1,0:T(8,128)}) async-done(((f32[128,256]{1,0:T(8,128)}, f32[256,128]{1,0:T(8,128)}), (f32[128,256]{1,0:T(8,128)}, f32[256,128]{1,0:T(8,128)})) %all-reduce.3.cloned.1.call-update) | async-done | bytes 262160 | tf_op jit(solution)/shard_map/psum | solution.py:87
  177.2 1.6 copy.50
  178.7 1.6 copy.51
  (93 shorter events, 9.8 us)
Async XLA Ops:
  7.2 13.1 %copy-start = (bf16[8192,128]{1,0:T(8,128)(2,1)S(1)}, bf16[8192,128]{1,0:T(8,128)(2,1)}, u32[]{:S(2)}) copy-start(bf16[8192,128]{1,0:T(8,128)(2,1)} %param.11) | copy-start | bytes 6291460
  7.2 170.0 %all-reduce.3.cloned.1.call-start = ((), (), s32[]{:S(2)}) async-start(), calls=%async_computation | async-start | bytes 524288 | tf_op jit(solution)/shard_map/psum | solution.py:87
  10.5 14.7 %collective-permute-start.10 = (s32[2]{0:T(128)S(1)}, s32[2]{0:T(128)S(1)}, u32[]{:S(2)}, u32[]{:S(2)}) collective-permute-start(s32[2]{0:T(128)S(1)} %get-tuple-element.37), channel_id=1, source_target_pairs={{0,3},{1,4},{2,5},{3,6},{4,7},{5,8},{6,9},{7,10},{8,11},{9,12},{10... | collective-permute-start | bytes 32 | tf_op jit(solution)/shard_map/ppermute | solution.py:12
  12.9 12.4 %collective-permute-start.8 = (s32[2]{0:T(128)S(1)}, s32[2]{0:T(128)S(1)}, u32[]{:S(2)}, u32[]{:S(2)}) collective-permute-start(s32[2]{0:T(128)S(1)} %get-tuple-element.38), channel_id=1, source_target_pairs={{0,2},{1,3},{2,4},{3,5},{4,6},{5,7},{6,8},{7,9},{8,10},{9,11},{10,... | collective-permute-start | bytes 32 | tf_op jit(solution)/shard_map/ppermute | solution.py:12
  14.4 11.0 %collective-permute-start.6 = (s32[2]{0:T(128)S(1)}, s32[2]{0:T(128)S(1)}, u32[]{:S(2)}, u32[]{:S(2)}) collective-permute-start(s32[2]{0:T(128)S(1)} %get-tuple-element.39), channel_id=1, source_target_pairs={{0,1},{1,2},{2,3},{3,4},{4,5},{5,6},{6,7},{7,8},{8,9},{9,10},{10,1... | collective-permute-start | bytes 32 | tf_op jit(solution)/shard_map/ppermute | solution.py:12
  14.8 10.5 %collective-permute-start.4 = (s32[2]{0:T(128)S(1)}, s32[2]{0:T(128)S(1)}, u32[]{:S(2)}, u32[]{:S(2)}) collective-permute-start(s32[2]{0:T(128)S(1)} %get-tuple-element.40), channel_id=1, source_target_pairs={{0,15},{1,0},{2,1},{3,2},{4,3},{5,4},{6,5},{7,6},{8,7},{9,8},{10,9... | collective-permute-start | bytes 32 | tf_op jit(solution)/shard_map/ppermute | solution.py:12
  18.8 6.6 %collective-permute-start.2 = (s32[2]{0:T(128)S(1)}, s32[2]{0:T(128)S(1)}, u32[]{:S(2)}, u32[]{:S(2)}) collective-permute-start(s32[2]{0:T(128)S(1)} %get-tuple-element.41), channel_id=1, source_target_pairs={{0,14},{1,15},{2,0},{3,1},{4,2},{5,3},{6,4},{7,5},{8,6},{9,7},{10,... | collective-permute-start | bytes 32 | tf_op jit(solution)/shard_map/ppermute | solution.py:12
  20.8 31.6 %copy-start.4 = (bf16[12,128,128]{2,1,0:T(8,128)(2,1)S(1)}, bf16[12,128,128]{2,1,0:T(8,128)(2,1)}, u32[]{:S(2)}) copy-start(bf16[12,128,128]{2,1,0:T(8,128)(2,1)} %param.14) | copy-start | bytes 1179652
  25.1 3.0 %collective-permute-start = (s32[2]{0:T(128)S(1)}, s32[2]{0:T(128)S(1)}, u32[]{:S(2)}, u32[]{:S(2)}) collective-permute-start(s32[2]{0:T(128)S(1)} %get-tuple-element.42), channel_id=1, source_target_pairs={{0,13},{1,14},{2,15},{3,0},{4,1},{5,2},{6,3},{7,4},{8,5},{9,6},{10... | collective-permute-start | bytes 32 | tf_op jit(solution)/shard_map/ppermute | solution.py:12
  31.6 18.4 %collective-permute-start.11 = (bf16[2,128,128]{2,1,0:T(8,128)(2,1)S(1)}, bf16[2,128,128]{2,1,0:T(8,128)(2,1)S(1)}, u32[]{:S(2)}, u32[]{:S(2)}) collective-permute-start(bf16[2,128,128]{2,1,0:T(8,128)(2,1)S(1)} %broadcast_select_fusion), channel_id=1, source_target_pairs={{0,13},{1,14},{2,15},{3,0},{4,1},{5,2},{6,3},{7,4},{8,5},{9,6},{10... | collective-permute-start | bytes 196616 | tf_op jit(solution)/shard_map/ppermute | solution.py:12
  33.6 16.4 %collective-permute-start.9 = (bf16[2,128,128]{2,1,0:T(8,128)(2,1)S(1)}, bf16[2,128,128]{2,1,0:T(8,128)(2,1)S(1)}, u32[]{:S(2)}, u32[]{:S(2)}) collective-permute-start(bf16[2,128,128]{2,1,0:T(8,128)(2,1)S(1)} %broadcast_select_fusion.1), channel_id=1, source_target_pairs={{0,14},{1,15},{2,0},{3,1},{4,2},{5,3},{6,4},{7,5},{8,6},{9,7},{10,... | collective-permute-start | bytes 196616 | tf_op jit(solution)/shard_map/ppermute | solution.py:12
  36.3 13.6 %collective-permute-start.7 = (bf16[2,128,128]{2,1,0:T(8,128)(2,1)S(1)}, bf16[2,128,128]{2,1,0:T(8,128)(2,1)S(1)}, u32[]{:S(2)}, u32[]{:S(2)}) collective-permute-start(bf16[2,128,128]{2,1,0:T(8,128)(2,1)S(1)} %broadcast_select_fusion.2), channel_id=1, source_target_pairs={{0,15},{1,0},{2,1},{3,2},{4,3},{5,4},{6,5},{7,6},{8,7},{9,8},{10,9... | collective-permute-start | bytes 196616 | tf_op jit(solution)/shard_map/ppermute | solution.py:12
  36.8 13.0 %collective-permute-start.5 = (bf16[2,128,128]{2,1,0:T(8,128)(2,1)S(1)}, bf16[2,128,128]{2,1,0:T(8,128)(2,1)S(1)}, u32[]{:S(2)}, u32[]{:S(2)}) collective-permute-start(bf16[2,128,128]{2,1,0:T(8,128)(2,1)S(1)} %broadcast_select_fusion.3), channel_id=1, source_target_pairs={{0,1},{1,2},{2,3},{3,4},{4,5},{5,6},{6,7},{7,8},{8,9},{9,10},{10,1... | collective-permute-start | bytes 196616 | tf_op jit(solution)/shard_map/ppermute | solution.py:12
  37.0 5.9 %collective-permute-start.1 = (bf16[2,128,128]{2,1,0:T(8,128)(2,1)S(1)}, bf16[2,128,128]{2,1,0:T(8,128)(2,1)S(1)}, u32[]{:S(2)}, u32[]{:S(2)}) collective-permute-start(bf16[2,128,128]{2,1,0:T(8,128)(2,1)S(1)} %broadcast_select_fusion.5), channel_id=1, source_target_pairs={{0,3},{1,4},{2,5},{3,6},{4,7},{5,8},{6,9},{7,10},{8,11},{9,12},{10... | collective-permute-start | bytes 196616 | tf_op jit(solution)/shard_map/ppermute | solution.py:12
  42.8 7.0 %collective-permute-start.3 = (bf16[2,128,128]{2,1,0:T(8,128)(2,1)S(1)}, bf16[2,128,128]{2,1,0:T(8,128)(2,1)S(1)}, u32[]{:S(2)}, u32[]{:S(2)}) collective-permute-start(bf16[2,128,128]{2,1,0:T(8,128)(2,1)S(1)} %broadcast_select_fusion.4), channel_id=1, source_target_pairs={{0,2},{1,3},{2,4},{3,5},{4,6},{5,7},{6,8},{7,9},{8,10},{9,11},{10,... | collective-permute-start | bytes 196616 | tf_op jit(solution)/shard_map/ppermute | solution.py:12
  50.0 0.8 copy-start.5
  55.2 5.8 %copy-start.6 = (bf16[128,256]{1,0:T(8,128)(2,1)S(1)}, bf16[128,256]{1,0:T(8,128)(2,1)}, u32[]{:S(2)}) copy-start(bf16[128,256]{1,0:T(8,128)(2,1)} %param.17) | copy-start | bytes 196612
  55.2 5.8 %copy-start.10 = (f32[256]{0:T(256)S(1)}, f32[256]{0:T(256)}, u32[]{:S(2)}) copy-start(f32[256]{0:T(256)} %param.18) | copy-start | bytes 3076
  61.0 1.3 copy-start.3
  61.0 2.3 %copy-start.2 = (bf16[8192,128]{1,0:T(8,128)(2,1)S(1)}, bf16[8192,128]{1,0:T(8,128)(2,1)}, u32[]{:S(2)}) copy-start(bf16[8192,128]{1,0:T(8,128)(2,1)} %param.12) | copy-start | bytes 6291460
  63.4 2.0 %copy-start.9 = (bf16[256,128]{1,0:T(8,128)(2,1)S(1)}, bf16[256,128]{1,0:T(8,128)(2,1)}, u32[]{:S(2)}) copy-start(bf16[256,128]{1,0:T(8,128)(2,1)} %param.19) | copy-start | bytes 196612
  67.2 2.7 %copy-start.1 = (bf16[8192,256]{1,0:T(8,128)(2,1)}, bf16[8192,256]{1,0:T(8,128)(2,1)S(1)}, u32[]{:S(2)}) copy-start(bf16[8192,256]{1,0:T(8,128)(2,1)S(1)} %get-tuple-element.44) | copy-start | bytes 12582916
  78.7 6.9 %copy-start.7 = (f32[2,128,128]{2,1,0:T(8,128)S(1)}, f32[2,128,128]{2,1,0:T(8,128)}, u32[]{:S(2)}) copy-start(f32[2,128,128]{2,1,0:T(8,128)} %get-tuple-element.27) | copy-start | bytes 393220
  78.7 10.9 %copy-start.8 = (f32[2,128,128]{2,1,0:T(8,128)S(1)}, f32[2,128,128]{2,1,0:T(8,128)}, u32[]{:S(2)}) copy-start(f32[2,128,128]{2,1,0:T(8,128)} %get-tuple-element.28) | copy-start | bytes 393220
  78.7 10.9 %collective-permute-start.12 = (f32[2,128,128]{2,1,0:T(8,128)}, f32[2,128,128]{2,1,0:T(8,128)S(1)}, u32[]{:S(2)}, u32[]{:S(2)}) collective-permute-start(f32[2,128,128]{2,1,0:T(8,128)} %get-tuple-element.29), channel_id=1, source_target_pairs={{0,13},{1,14},{2,15},{3,0},{4,1},{5,2},{6,3},{7,4},{8,5},{9,6},{10... | collective-permute-start | bytes 393224 | tf_op jit(solution)/shard_map/ppermute | solution.py:12
  83.1 61.6 %collective-permute-start.17 = (f32[2,128,128]{2,1,0:T(8,128)S(1)}, f32[2,128,128]{2,1,0:T(8,128)S(1)}, u32[]{:S(2)}, u32[]{:S(2)}) collective-permute-start(f32[2,128,128]{2,1,0:T(8,128)S(1)} %get-tuple-element.23), channel_id=1, source_target_pairs={{0,3},{1,4},{2,5},{3,6},{4,7},{5,8},{6,9},{7,10},{8,11},{9,12},{10... | collective-permute-start | bytes 393224 | tf_op jit(solution)/shard_map/ppermute | solution.py:12
  84.8 57.8 %collective-permute-start.16 = (f32[2,128,128]{2,1,0:T(8,128)S(1)}, f32[2,128,128]{2,1,0:T(8,128)S(1)}, u32[]{:S(2)}, u32[]{:S(2)}) collective-permute-start(f32[2,128,128]{2,1,0:T(8,128)S(1)} %get-tuple-element.24), channel_id=1, source_target_pairs={{0,2},{1,3},{2,4},{3,5},{4,6},{5,7},{6,8},{7,9},{8,10},{9,11},{10,... | collective-permute-start | bytes 393224 | tf_op jit(solution)/shard_map/ppermute | solution.py:12
  84.8 56.1 %collective-permute-start.15 = (f32[2,128,128]{2,1,0:T(8,128)S(1)}, f32[2,128,128]{2,1,0:T(8,128)S(1)}, u32[]{:S(2)}, u32[]{:S(2)}) collective-permute-start(f32[2,128,128]{2,1,0:T(8,128)S(1)} %get-tuple-element.25), channel_id=1, source_target_pairs={{0,1},{1,2},{2,3},{3,4},{4,5},{5,6},{6,7},{7,8},{8,9},{9,10},{10,1... | collective-permute-start | bytes 393224 | tf_op jit(solution)/shard_map/ppermute | solution.py:12
  85.6 51.1 %collective-permute-start.14 = (f32[2,128,128]{2,1,0:T(8,128)S(1)}, f32[2,128,128]{2,1,0:T(8,128)S(1)}, u32[]{:S(2)}, u32[]{:S(2)}) collective-permute-start(f32[2,128,128]{2,1,0:T(8,128)S(1)} %copy-done.7), channel_id=1, source_target_pairs={{0,15},{1,0},{2,1},{3,2},{4,3},{5,4},{6,5},{7,6},{8,7},{9,8},{10,9... | collective-permute-start | bytes 393224 | tf_op jit(solution)/shard_map/ppermute | solution.py:12
  89.7 44.6 %collective-permute-start.13 = (f32[2,128,128]{2,1,0:T(8,128)S(1)}, f32[2,128,128]{2,1,0:T(8,128)}, u32[]{:S(2)}, u32[]{:S(2)}) collective-permute-start(f32[2,128,128]{2,1,0:T(8,128)S(1)} %copy-done.8), channel_id=1, source_target_pairs={{0,14},{1,15},{2,0},{3,1},{4,2},{5,3},{6,4},{7,5},{8,6},{9,7},{10,... | collective-permute-start | bytes 393224 | tf_op jit(solution)/shard_map/ppermute | solution.py:12
Sparse Core Ops, SparseCore 0:
  89.8 87.3 all-reduce.2
where the time goes:
time: 189 us; the launch traced here: 187 us
  waiting for transfers between devices  35.1 us (19%)
  other arithmetic  30.9 us (16%)
  blocking collectives  30.1 us (16%)
  starting transfers between devices  27.6 us (15%)
  matrix products  24.2 us (13%)
  local copies, waits for them, and re-layouts  24 us (13%)
  between operations  15.3 us (8%)
    psum x1, blocking collectives, body(): d_in, d_b, d_out = lax.psum((d_in, d_b, d_out), 'lon')  30.1 us
    ppermute x18, starting transfers between devices, from_behind(): lax.ppermute(array, axis, [(i, (i + by) % count) for i in range(count)])  27.6 us
    psum x1, waiting for transfers between devices, body(): d_in, d_b, d_out = lax.psum((d_in, d_b, d_out), 'lon')  27.1 us
    scatter-add x7, other arithmetic, body(): total = total.at[owners_rows].add(returned, mode='drop')  14 us
    ppermute x18, waiting for transfers between devices, from_behind(): lax.ppermute(array, axis, [(i, (i + by) % count) for i in range(count)])  7.98 us
    dot_general x1, local copies, waits for them, and re-layouts, body(): jnp.einsum('tdc,tdf->tcf', local_interp, gy_b, preferred_element_type=jnp...  5.61 us
    unnamed x29, local copies, waits for them, and re-layouts  5.1 us
    dot_general x1, matrix products, body(): jnp.einsum('tdc,tdf->tcf', local_interp, gy_b, preferred_element_type=jnp...  5.07 us
  transfers between devices with their start and end apart: 19, of which 3 were waited for; matrix products, arithmetic and copies ran while one was open for 22% of the time, Pallas kernels for 0%

commit v1 on v0

v1 whole, which is shorter than its diff:
```python
import functools

import jax
import jax.numpy as jnp
from jax import lax
from jax.experimental import pallas as pl
from jax.experimental.pallas import tpu as pltpu
from jax.sharding import PartitionSpec as P

CAP = 2
REACH = 3
SPAN = 2 * REACH + 1
SLOTS = SPAN * CAP
GROUP = 16
CHUNK = 4
MESH = pl.DeviceIdType.MESH
F32 = jnp.float32
BF16 = jnp.bfloat16


def mm(a, b):
    return jnp.dot(a, b, preferred_element_type=F32)


def mm_nt(a, b):
    return lax.dot_general(a, b, (((1,), (1,)), ((), ())), preferred_element_type=F32)


def mm_tn(a, b):
    return lax.dot_general(a, b, (((0,), (0,)), ((), ())), preferred_element_type=F32)


def kernel(
    tiles,
    dep, cnt, w_in, b_in, w_out, state_h, cot_h, local_h, remote_h,
    grad_h, din_o, db_o, dout_o,
    state, cot, local, remote, gy, back, result,
    sendbox, fetched, outbox, returned, acc, racc, ysp, csp,
    gsum, dbsum, gout, gin, red, gall, dbin, xin,
    ask_out, ask_in, spec_v, own_v,
    ask_s, spec_s, own_s, spot_s, prev_s, ent_s, last_s,
    in_sem, chunk_sem, out_sem, small_sem,
    ask_send, ask_recv, fet_send, fet_recv, ret_send, ret_recv,
    rs_send, rs_recv, db_send, db_recv, ag_send, ag_recv, x_send, x_recv,
):
    nblocks, width, feat = state.shape
    entries = remote.shape[0]
    nchunks = nblocks // CHUNK
    rows = CHUNK * width
    me = lax.axis_index("lon")
    group = min(GROUP, tiles)
    groups = tiles // group
    part = gout.shape[1]

    def peer_at(offset):
        return lax.rem(me + offset + tiles, tiles)

    load_state = pltpu.make_async_copy(state_h, state, in_sem.at[0])
    load_remote = pltpu.make_async_copy(remote_h, remote, in_sem.at[1])
    load_state.start()

    def load_chunk(c):
        at = pl.ds(c * CHUNK, CHUNK)
        return (
            pltpu.make_async_copy(local_h.at[at], local.at[at], chunk_sem.at[0, c]),
            pltpu.make_async_copy(cot_h.at[at], cot.at[at], chunk_sem.at[1, c]),
        )

    @pl.loop(0, nchunks)
    def _(c):
        for copy in load_chunk(c):
            copy.start()

    load_remote.start()

    barrier = pltpu.get_barrier_semaphore()

    @pl.loop(1, tiles)
    def _(i):
        pl.semaphore_signal(barrier, inc=1, device_id={"lon": peer_at(i)}, device_id_type=MESH)

    count = cnt[0]
    keys, dests, spots = [], [], []
    for e in range(entries):
        ahead = dep[0, e] - me + REACH
        ahead = jnp.where(ahead < 0, ahead + tiles, ahead)
        ahead = jnp.where(ahead >= tiles, ahead - tiles, ahead)
        alive = e < count
        keys.append(jnp.where(alive, ahead, -1))
        dests.append(jnp.where(alive, dep[2, e], -1))
        rank = jnp.int32(0)
        prev = jnp.int32(0)
        for q in range(e):
            rank = rank + jnp.where(keys[q] == keys[e], 1, 0)
            prev = jnp.where(dests[q] == dests[e], q + 1, prev)
        spots.append(jnp.where(alive, ahead * CAP + rank, SLOTS))
        spot_s[e] = spots[e]
        prev_s[e] = prev
    line = lax.broadcasted_iota(jnp.int32, (8, 128), 0)
    lane = lax.broadcasted_iota(jnp.int32, (8, 128), 1)
    tile = jnp.full((8, 128), -1, jnp.int32)
    place = jnp.where(lane < CAP, line * CAP + lane, -1)
    slot_entry = jnp.full((8, 128), entries, jnp.int32)
    special = jnp.zeros((8, 128), jnp.int32)
    for e in range(entries):
        tile = jnp.where(place == spots[e], dep[1, e], tile)
        slot_entry = jnp.where(lane == spots[e], e, slot_entry)
        special = jnp.where(lane == dests[e], e + 1, special)
    ask_out[...] = tile
    ask_in[REACH] = tile
    spec_v[0] = special
    spec_v[1] = slot_entry
    spec_copy = pltpu.make_async_copy(spec_v, spec_s, small_sem.at[0])
    spec_copy.start()
    acc[0] = jnp.zeros((width, feat), F32)
    racc[0] = jnp.zeros((width, feat), F32)
    gsum[...] = jnp.zeros_like(gsum)
    dbsum[...] = jnp.zeros_like(dbsum)

    pl.semaphore_wait(barrier, tiles - 1)

    def ask_copy(r):
        return pltpu.make_async_remote_copy(
            src_ref=ask_out, dst_ref=ask_in.at[r],
            send_sem=ask_send.at[r], recv_sem=ask_recv.at[r],
            device_id={"lon": peer_at(r - REACH)}, device_id_type=MESH)

    def fetch_copy(r):
        at = pl.ds(r * CAP, CAP)
        return pltpu.make_async_remote_copy(
            src_ref=sendbox.at[at], dst_ref=fetched.at[at],
            send_sem=fet_send.at[r], recv_sem=fet_recv.at[r],
            device_id={"lon": peer_at(REACH - r)}, device_id_type=MESH)

    def return_copy(r):
        at = pl.ds(r * CAP, CAP)
        return pltpu.make_async_remote_copy(
            src_ref=outbox.at[at], dst_ref=returned.at[at],
            send_sem=ret_send.at[r], recv_sem=ret_recv.at[r],
            device_id={"lon": peer_at(r - REACH)}, device_id_type=MESH)

    others = [r for d in range(REACH, 0, -1) for r in (REACH - d, REACH + d)]
    for r in others:
        ask_copy(r).start()

    def network(y32, ct_ref, base, marks):
        y_b = y32.astype(BF16)
        ct = ct_ref[pl.ds(base, CHUNK)].reshape(rows, feat)
        pre = mm(y_b, w_in[...]) + b_in[...]
        hidden = jnp.tanh(pre)
        h_b = hidden.astype(BF16)
        ghid = mm_nt(ct, w_out[...])
        gpre = ghid * (1.0 - hidden * hidden)
        gpre_b = gpre.astype(BF16)
        ct32 = ct.astype(F32)
        out = (ct32 + mm_nt(gpre_b, w_in[...])).astype(BF16)
        y_m, ct_m, db = [], [], None
        for i in range(CHUNK):
            at = slice(i * width, (i + 1) * width)
            y_m.append((y32[at] * marks[i]).astype(BF16))
            ct_m.append((ct32[at] * marks[i]).astype(BF16))
            here = jnp.sum(gpre[at].reshape(width // 8, 8, -1), axis=0) * marks[i]
            db = here if db is None else db + here
        gsum[:feat] += mm_tn(jnp.concatenate(y_m, axis=0), gpre_b)
        gsum[feat:] += mm_tn(jnp.concatenate(ct_m, axis=0), h_b)
        dbsum[...] += db
        return out.reshape(CHUNK, width, feat)

    def step(c, carry):
        for copy in load_chunk(c):
            copy.wait()
        y, marks = [], []
        for i in range(CHUNK):
            t = c * CHUNK + i
            y.append(mm(local[t], state[t]))
            marks.append(jnp.where(spec_s[0, 0, t] == 0, 1.0, 0.0).astype(F32))
        gy[pl.ds(c * CHUNK, CHUNK)] = network(jnp.concatenate(y, axis=0), cot, c * CHUNK, marks)
        return carry

    spec_copy.wait()
    load_state.wait()
    first = min(2, nchunks)
    second = min(3, nchunks)
    lax.fori_loop(0, first, step, 0)

    for r in others:
        ask_copy(r).wait_recv()
    asked_copy = pltpu.make_async_copy(ask_in, ask_s, small_sem.at[1])
    asked_copy.start()
    lax.fori_loop(first, second, step, 0)
    asked_copy.wait()

    asked = []
    for r in range(SPAN):
        for c in range(CAP):
            asked.append(ask_s[r, r, c])
    for r in others + [REACH]:
        for c in range(CAP):
            k = r * CAP + c
            block = state[jnp.clip(asked[k], 0, nblocks - 1)]
            if r == REACH:
                fetched[k] = block
            else:
                sendbox[k] = block
        if r != REACH:
            fetch_copy(r).start()
    owners = jnp.zeros((8, 128), jnp.int32)
    for k in range(SLOTS):
        last = jnp.int32(0)
        for q in range(k):
            last = jnp.where(asked[q] == asked[k], q + 1, last)
        last_s[k] = last
        owners = jnp.where(lane == asked[k], k + 1, owners)
    own_v[...] = owners
    own_copy = pltpu.make_async_copy(own_v, own_s, small_sem.at[2])
    own_copy.start()

    lax.fori_loop(second, nchunks, step, 0)

    load_remote.wait()
    for r in others:
        fetch_copy(r).wait_recv()

    @pl.loop(0, entries)
    def _(e):
        spot = spot_s[e]
        weight = jnp.where(spot < SLOTS, 1.0, 0.0).astype(F32)
        total = mm(remote[e], fetched[jnp.minimum(spot, SLOTS - 1)]) * weight + acc[prev_s[e]]
        acc[e + 1] = total
        d = dep[2, e]
        ysp[e] = mm(local[d], state[d]) + total
        csp[e] = cot[d]

    @pl.loop(0, entries // CHUNK)
    def _(c):
        marks = []
        for i in range(CHUNK):
            e = c * CHUNK + i
            marks.append(jnp.where(spec_s[0, 0, dep[2, e]] == e + 1, 1.0, 0.0).astype(F32))
        y32 = ysp[pl.ds(c * CHUNK, CHUNK)].reshape(rows, feat)
        gy[pl.ds(nblocks + c * CHUNK, CHUNK)] = network(y32, csp, c * CHUNK, marks)

    for r in others + [REACH]:
        for c in range(CAP):
            k = r * CAP + c
            e = jnp.minimum(spec_s[1, 0, k], entries - 1)
            at = jnp.maximum(spec_s[0, 0, dep[2, e]] - 1, 0) + nblocks
            value = mm_tn(remote[e], gy[at]).astype(BF16)
            if r == REACH:
                returned[k] = value
            else:
                outbox[k] = value
        if r != REACH:
            return_copy(r).start()

    mine = lax.rem(me, group)
    base = me - mine
    gout[...] = gsum[...].astype(BF16).reshape(gout.shape)
    dbin[me] = jnp.sum(dbsum[...], axis=0, keepdims=True)

    def mate(i):
        return lax.rem(mine + i, group)

    def share_copy(i):
        return pltpu.make_async_remote_copy(
            src_ref=gout.at[mate(i)], dst_ref=gin.at[i],
            send_sem=rs_send.at[i], recv_sem=rs_recv.at[i],
            device_id={"lon": base + mate(i)}, device_id_type=MESH)

    def bias_copy(i):
        return pltpu.make_async_remote_copy(
            src_ref=dbin.at[me], dst_ref=dbin.at[me],
            send_sem=db_send.at[i], recv_sem=db_recv.at[i],
            device_id={"lon": peer_at(i)}, device_id_type=MESH)

    def gather_copy(i):
        return pltpu.make_async_remote_copy(
            src_ref=red, dst_ref=gall.at[mine],
            send_sem=ag_send.at[i], recv_sem=ag_recv.at[i],
            device_id={"lon": base + mate(i)}, device_id_type=MESH)

    def cross_copy(i):
        return pltpu.make_async_remote_copy(
            src_ref=xin.at[me // group], dst_ref=xin.at[me // group],
            send_sem=x_send.at[i], recv_sem=x_recv.at[i],
            device_id={"lon": peer_at(i * group)}, device_id_type=MESH)

    @pl.loop(1, group)
    def _(i):
        share_copy(i).start()

    @pl.loop(1, tiles)
    def _(i):
        bias_copy(i).start()

    @pl.loop(0, nchunks)
    def _(c):
        for i in range(CHUNK):
            t = c * CHUNK + i
            s = spec_s[0, 0, t]
            back[t] = mm_tn(local[t], gy[jnp.where(s == 0, t, nblocks + s - 1)])

    @pl.loop(1, group)
    def _(i):
        share_copy(i).wait_recv()

    share = gsum[pl.ds(pl.multiple_of(mine * part, part), part)]
    share = lax.fori_loop(1, group, lambda i, s: s + gin[i].astype(F32), share)
    if groups > 1:
        xin[me // group] = share.astype(BF16)

        @pl.loop(1, groups)
        def _(i):
            cross_copy(i).start()

        @pl.loop(1, groups)
        def _(i):
            cross_copy(i).wait()

        share = lax.fori_loop(
            0, groups, lambda i, s: s + xin[i].astype(F32), jnp.zeros(share.shape, F32))
    red[...] = share.astype(BF16)
    gall[mine] = share.astype(BF16)

    @pl.loop(1, group)
    def _(i):
        gather_copy(i).start()

    own_copy.wait()
    for r in others:
        return_copy(r).wait_recv()
    for k in range(SLOTS):
        weight = jnp.where(asked[k] >= 0, 1.0, 0.0).astype(F32)
        racc[k + 1] = returned[k].astype(F32) * weight + racc[last_s[k]]

    def store_chunk(c):
        at = pl.ds(c * CHUNK, CHUNK)
        return pltpu.make_async_copy(result.at[at], grad_h.at[at], out_sem.at[c])

    @pl.loop(0, nchunks)
    def _(c):
        for i in range(CHUNK):
            t = c * CHUNK + i
            result[t] = (back[t] + racc[own_s[0, t]]).astype(BF16)
        store_chunk(c).start()

    @pl.loop(1, tiles)
    def _(i):
        bias_copy(i).wait()

    db_o[...] = lax.fori_loop(1, tiles, lambda i, s: s + dbin[i], dbin[0])

    @pl.loop(1, group)
    def _(i):
        share_copy(i).wait_send()
        gather_copy(i).wait()

    whole = gall[...].astype(F32).reshape(2 * feat, -1)
    din_o[...] = whole[:feat]
    dout_o[...] = whole[feat:].T

    for r in others:
        ask_copy(r).wait_send()
        fetch_copy(r).wait_send()
        return_copy(r).wait_send()

    @pl.loop(0, nchunks)
    def _(c):
        store_chunk(c).wait()


def body(tiles, state, cotangent, local_interp, remote_interp, departures, counts, w_in, b_in, w_out):
    nblocks, width, _ = local_interp.shape
    feat = state.shape[1]
    hid = w_in.shape[1]
    entries = remote_interp.shape[0]
    nchunks = nblocks // CHUNK
    group = min(GROUP, tiles)
    part = 2 * feat // group
    dma = pltpu.SemaphoreType.DMA
    vmem = pl.BlockSpec(memory_space=pltpu.VMEM)
    smem = pl.BlockSpec(memory_space=pltpu.SMEM)
    hbm = pl.BlockSpec(memory_space=pl.ANY)
    blk = (width, feat)
    grad, d_in, d_b, d_out = pl.pallas_call(
        functools.partial(kernel, tiles),
        out_shape=(
            jax.ShapeDtypeStruct((nblocks,) + blk, BF16),
            jax.ShapeDtypeStruct((feat, hid), F32),
            jax.ShapeDtypeStruct((1, hid), F32),
            jax.ShapeDtypeStruct((hid, feat), F32),
        ),
        in_specs=[smem, smem, vmem, vmem, vmem, hbm, hbm, hbm, hbm],
        out_specs=(hbm, vmem, vmem, vmem),
        scratch_shapes=[
            pltpu.VMEM((nblocks,) + blk, BF16),
            pltpu.VMEM((nblocks,) + blk, BF16),
            pltpu.VMEM((nblocks, width, width), BF16),
            pltpu.VMEM((entries, width, width), BF16),
            pltpu.VMEM((nblocks + entries,) + blk, BF16),
            pltpu.VMEM((nblocks,) + blk, F32),
            pltpu.VMEM((nblocks,) + blk, BF16),
            pltpu.VMEM((SLOTS,) + blk, BF16),
            pltpu.VMEM((SLOTS,) + blk, BF16),
            pltpu.VMEM((SLOTS,) + blk, BF16),
            pltpu.VMEM((SLOTS,) + blk, BF16),
            pltpu.VMEM((entries + 1,) + blk, F32),
            pltpu.VMEM((SLOTS + 1,) + blk, F32),
            pltpu.VMEM((entries,) + blk, F32),
            pltpu.VMEM((entries,) + blk, BF16),
            pltpu.VMEM((2 * feat, hid), F32),
            pltpu.VMEM((8, hid), F32),
            pltpu.VMEM((group, part, hid), BF16),
            pltpu.VMEM((group, part, hid), BF16),
            pltpu.VMEM((part, hid), BF16),
            pltpu.VMEM((group, part, hid), BF16),
            pltpu.VMEM((tiles, 1, hid), F32),
            pltpu.VMEM((tiles // group, part, hid), BF16),
            pltpu.VMEM((8, 128), jnp.int32),
            pltpu.VMEM((SPAN, 8, 128), jnp.int32),
            pltpu.VMEM((2, 8, 128), jnp.int32),
            pltpu.VMEM((8, 128), jnp.int32),
            pltpu.SMEM((SPAN, 8, 128), jnp.int32),
            pltpu.SMEM((2, 8, 128), jnp.int32),
            pltpu.SMEM((8, 128), jnp.int32),
            pltpu.SMEM((entries,), jnp.int32),
            pltpu.SMEM((entries,), jnp.int32),
            pltpu.SMEM((SLOTS,), jnp.int32),
            pltpu.SMEM((SLOTS,), jnp.int32),
            dma((2,)), dma((2, nchunks)), dma((nchunks,)), dma((3,)),
            dma((SPAN,)), dma((SPAN,)), dma((SPAN,)), dma((SPAN,)), dma((SPAN,)), dma((SPAN,)),
            dma((group,)), dma((group,)), dma((tiles,)), dma((tiles,)),
            dma((group,)), dma((group,)),
            dma((max(tiles // group, 2),)), dma((max(tiles // group, 2),)),
        ],
        compiler_params=pltpu.CompilerParams(
            collective_id=0, has_side_effects=True, vmem_limit_bytes=48 * 1024 * 1024
        ),
    )(
        departures, counts, w_in, b_in.reshape(1, hid), w_out,
        state.reshape(nblocks, width, feat), cotangent.reshape(nblocks, width, feat),
        local_interp, remote_interp,
    )
    return grad.reshape(nblocks * width, feat), d_in, d_b.reshape(hid), d_out


def solution(mesh):
    return jax.shard_map(
        functools.partial(body, mesh.shape["lon"]),
        mesh=mesh,
        in_specs=(
            P(("members", "lon"), None),
            P(("members", "lon"), None),
            P(("members", "lon"), None, None),
            P(("members", "lon"), None, None),
            P(None, ("members", "lon")),
            P(("members", "lon")),
            P(),
            P(),
            P(),
        ),
        out_specs=(
            P(("members", "lon"), None),
            P("members", None),
            P("members"),
            P("members", None),
        ),
        check_vma=False,
    )
```

time: 189 us -> 49.9 us (0.26)
  Pallas kernels: 0 us -> 39.4 us
  waiting for transfers between devices: 35.1 us -> 0 us
  other arithmetic: 30.9 us -> 0 us
  blocking collectives: 30.1 us -> 0 us
  starting transfers between devices: 27.6 us -> 0 us
  matrix products: 24.2 us -> 0 us
  local copies, waits for them, and re-layouts: 24 us -> 8.81 us
  between operations: 15.3 us -> 1.3 us
    pallas_call x0 -> x1, Pallas kernels: none -> 39.4 us  [body(): pl.pallas_call(functools.partial(kernel, tiles), out_shape=(jax.ShapeDtyp...]
    psum x1 -> x0, blocking collectives: 30.1 us -> none  [body(): d_in, d_b, d_out = lax.psum((d_in, d_b, d_out), 'lon')]
    ppermute x18 -> x0, starting transfers between devices: 27.6 us -> none  [from_behind(): lax.ppermute(array, axis, [(i, (i + by) % count) for i in range(count)])]
    psum x1 -> x0, waiting for transfers between devices: 27.1 us -> none  [body(): d_in, d_b, d_out = lax.psum((d_in, d_b, d_out), 'lon')]
    dot_general x9 -> x0, matrix products: 24.2 us -> none  [the longest x1 5.07 us: body(): jnp.einsum('tdc,tdf->tcf', local_interp, gy_b, preferred_element_type=jnp...]
    scatter-add x9 -> x0, other arithmetic: 19.7 us -> none  [the longest x7 14 us: body(): total = total.at[owners_rows].add(returned, mode='drop')]
    gather x9 -> x0, local copies, waits for them, and re-layouts: 8.53 us -> none  [the longest x7 3.95 us: body(): outgoing = jnp.take(blocks, jnp.clip(asked_here, 0, nblocks - 1), axis=0)]
    ppermute x18 -> x0, waiting for transfers between devices: 7.98 us -> none  [from_behind(): lax.ppermute(array, axis, [(i, (i + by) % count) for i in range(count)])]
  transfers between devices with their start and end apart: 19 -> 0, of which waited for: 3 -> 0; matrix products, arithmetic and copies ran while one was open for 22% -> 0% of each run, Pallas kernels for 0% -> 0%
where the time goes in v1:
time: 49.9 us; the launch traced here: 49.5 us
  Pallas kernels  39.4 us (79%)
  local copies, waits for them, and re-layouts  8.81 us (18%)
  between operations  1.3 us (3%)
    pallas_call x1, Pallas kernels, body(): pl.pallas_call(functools.partial(kernel, tiles), out_shape=(jax.ShapeDtyp...  39.4 us
    unnamed x16, local copies, waits for them, and re-layouts  8.81 us

profile of v1, /device:TPU:0, one launch (start us, length us, event | category | flops | bytes accessed | tf_op | source)
XLA Modules:
  0.0 49.5 jit_solution(9523412233839494562)
XLA Ops:
  1.3 0.0 copy-start
  1.3 1.6 %copy-done = bf16[8192,128]{1,0:T(8,128)(2,1)S(1)} copy-done((bf16[8192,128]{1,0:T(8,128)(2,1)S(1)}, bf16[8192,128]{1,0:T(8,128)(2,1)}, u32[]{:S(2)}) %copy-start) | copy-done | bytes 2097176
  2.9 0.0 copy-start.1
  2.9 1.0 %copy-done.1 = bf16[12,128,128]{2,1,0:T(8,128)(2,1)S(1)} copy-done((bf16[12,128,128]{2,1,0:T(8,128)(2,1)S(1)}, bf16[12,128,128]{2,1,0:T(8,128)(2,1)}, u32[]{:S(2)}) %copy-start.1) | copy-done | bytes 393240
  3.9 0.0 copy-start.2
  3.9 0.8 %copy-done.2 = bf16[128,256]{1,0:T(8,128)(2,1)S(1)} copy-done((bf16[128,256]{1,0:T(8,128)(2,1)S(1)}, bf16[128,256]{1,0:T(8,128)(2,1)}, u32[]{:S(2)}) %copy-start.2) | copy-done | bytes 65560
  4.7 0.0 copy-start.3
  4.7 0.8 %copy-done.3 = bf16[256,128]{1,0:T(8,128)(2,1)S(1)} copy-done((bf16[256,128]{1,0:T(8,128)(2,1)S(1)}, bf16[256,128]{1,0:T(8,128)(2,1)}, u32[]{:S(2)}) %copy-start.3) | copy-done | bytes 65560
  5.5 0.0 copy-start.4
  5.5 0.7 %copy-done.4 = s32[3,12]{1,0:T(4,128)S(1)} copy-done((s32[3,12]{1,0:T(4,128)S(1)}, s32[3,12]{1,0:T(4,128)}, u32[]{:S(2)}) %copy-start.4) | copy-done | bytes 168
  6.2 0.0 copy-start.5
  6.2 0.7 %copy-done.5 = f32[256]{0:T(256)S(1)} copy-done((f32[256]{0:T(256)S(1)}, f32[256]{0:T(256)}, u32[]{:S(2)}) %copy-start.5) | copy-done | bytes 1048
  6.9 39.4 %shard_map.120 = (bf16[64,128,128]{2,1,0:T(8,128)(2,1)S(1)}, f32[128,256]{1,0:T(8,128)S(1)}, f32[1,256]{1,0:T(1,128)S(1)}, f32[256,128]{1,0:T(8,128)S(1)}) custom-call(s32[3,12]{1,0:T(4,128)S(1)} %copy-done.4, s32[1]{0:T(128)S(6)} %copy.17.cnt, bf16[128,256]{1,0:T(8,128)(2,1)S(1)} %copy-done.2, f32[1,256]{1,0:T(1,128)S(1)} %bitcast.8, ...), custom_call_target="tpu_custom_call" | custom-call | tf_op jit(solution)/shard_map/pallas_call | solution.py:385
  46.3 1.3 %copy.18 = bf16[8192,128]{1,0:T(8,128)(2,1)} copy(bf16[8192,128]{1,0:T(8,128)(2,1)S(1)} %bitcast.5) | data formatting | bytes 4194304
  47.7 0.7 %copy.19 = f32[128,256]{1,0:T(8,128)} copy(f32[128,256]{1,0:T(8,128)S(1)} %get-tuple-element.17) | data formatting | bytes 262144
  48.3 0.6 %copy.20 = f32[256]{0:T(256)} copy(f32[256]{0:T(256)S(1)} %bitcast.7) | data formatting | bytes 2048
  48.9 0.7 %copy.21 = f32[256,128]{1,0:T(8,128)} copy(f32[256,128]{1,0:T(8,128)S(1)} %get-tuple-element.19) | data formatting | bytes 262144
Async XLA Ops:
  1.3 1.6 %copy-start = (bf16[8192,128]{1,0:T(8,128)(2,1)S(1)}, bf16[8192,128]{1,0:T(8,128)(2,1)}, u32[]{:S(2)}) copy-start(bf16[8192,128]{1,0:T(8,128)(2,1)} %param.9) | copy-start | bytes 6291460
  2.9 1.0 %copy-start.1 = (bf16[12,128,128]{2,1,0:T(8,128)(2,1)S(1)}, bf16[12,128,128]{2,1,0:T(8,128)(2,1)}, u32[]{:S(2)}) copy-start(bf16[12,128,128]{2,1,0:T(8,128)(2,1)} %remote_h.1) | copy-start | bytes 1179652
  3.9 0.8 %copy-start.2 = (bf16[128,256]{1,0:T(8,128)(2,1)S(1)}, bf16[128,256]{1,0:T(8,128)(2,1)}, u32[]{:S(2)}) copy-start(bf16[128,256]{1,0:T(8,128)(2,1)} %w_in.1) | copy-start | bytes 196612
  4.7 0.8 %copy-start.3 = (bf16[256,128]{1,0:T(8,128)(2,1)S(1)}, bf16[256,128]{1,0:T(8,128)(2,1)}, u32[]{:S(2)}) copy-start(bf16[256,128]{1,0:T(8,128)(2,1)} %w_out.1) | copy-start | bytes 196612
  5.5 0.7 %copy-start.4 = (s32[3,12]{1,0:T(4,128)S(1)}, s32[3,12]{1,0:T(4,128)}, u32[]{:S(2)}) copy-start(s32[3,12]{1,0:T(4,128)} %dep.1) | copy-start | bytes 436
  6.2 0.7 %copy-start.5 = (f32[256]{0:T(256)S(1)}, f32[256]{0:T(256)}, u32[]{:S(2)}) copy-start(f32[256]{0:T(256)} %param.16) | copy-start | bytes 3076

commit v2 on v1

v2 whole, which is shorter than its diff:
```python
import functools

import jax
import jax.numpy as jnp
from jax import lax
from jax.experimental import pallas as pl
from jax.experimental.pallas import tpu as pltpu
from jax.sharding import PartitionSpec as P

CAP = 2
REACH = 3
SPAN = 2 * REACH + 1
OFFSETS = [0] + [sign * d for d in range(1, REACH + 1) for sign in (-1, 1)]
SLOTS = SPAN * CAP
GROUP = 16
CHUNK = 4
MESH = pl.DeviceIdType.MESH
F32 = jnp.float32
BF16 = jnp.bfloat16


def mm(a, b):
    return jnp.dot(a, b, preferred_element_type=F32)


def mm_nt(a, b):
    return lax.dot_general(a, b, (((1,), (1,)), ((), ())), preferred_element_type=F32)


def mm_tn(a, b):
    return lax.dot_general(a, b, (((0,), (0,)), ((), ())), preferred_element_type=F32)


def kernel(
    tiles,
    dep_h, cnt_h, w_in_h, b_in_h, w_out_h, state_h, cot_h, local_h, remote_h,
    blocks_h, choice_h, din_h, db_h, dout_h,
    w_in, b_in, w_out, state, cot, local, remote, gy, result, patch,
    sendbox, fetched, outbox, returned, acc, racc, ysp, csp,
    gsum, dbsum, gout, gin, red, gall, dbin, xin, din, db, dout,
    ask_out, ask_in, spec_v, choice_v,
    dep, cnt, ask_s, spec_s, spot_s, prev_s,
    in_sem, chunk_sem, out_sem, end_sem, small_sem,
    ask_send, ask_recv, fet_send, fet_recv, ret_send, ret_recv,
    rs_send, rs_recv, db_send, db_recv, ag_send, ag_recv, x_send, x_recv,
):
    nblocks, width, feat = state.shape
    entries = remote.shape[0]
    nchunks = nblocks // CHUNK
    me = lax.axis_index("lon")
    group = min(GROUP, tiles)
    groups = tiles // group
    part = gout.shape[1]

    def peer_at(offset):
        return lax.rem(me + offset + tiles, tiles)

    loads = [
        pltpu.make_async_copy(src, dst, in_sem.at[n])
        for n, (src, dst) in enumerate([
            (dep_h, dep), (cnt_h, cnt), (state_h, state), (w_in_h, w_in), (b_in_h, b_in),
            (w_out_h, w_out), (remote_h, remote)])
    ]
    for copy in loads[:6]:
        copy.start()

    barrier = pltpu.get_barrier_semaphore()

    @pl.loop(1, tiles)
    def _(i):
        pl.semaphore_signal(barrier, inc=1, device_id={"lon": peer_at(i)}, device_id_type=MESH)

    def load_chunk(c):
        at = pl.ds(c * CHUNK, CHUNK)
        return (
            pltpu.make_async_copy(local_h.at[at], local.at[at], chunk_sem.at[0, c]),
            pltpu.make_async_copy(cot_h.at[at], cot.at[at], chunk_sem.at[1, c]),
        )

    @pl.loop(0, nchunks)
    def _(c):
        for copy in load_chunk(c):
            copy.start()

    loads[6].start()
    acc[0] = jnp.zeros((width, feat), F32)
    gsum[...] = jnp.zeros_like(gsum)
    dbsum[...] = jnp.zeros_like(dbsum)
    loads[0].wait()
    loads[1].wait()

    count = cnt[0]
    dests, spots = [], []
    line = lax.broadcasted_iota(jnp.int32, (8, 128), 0)
    lane = lax.broadcasted_iota(jnp.int32, (8, 128), 1)
    tile = jnp.full((8, 128), -1, jnp.int32)
    place = jnp.where(lane < CAP, line * CAP + lane, -1)
    slot_entry = jnp.full((8, 128), entries, jnp.int32)
    special = jnp.zeros((8, 128), jnp.int32)
    keys = []
    for e in range(entries):
        ahead = dep[0, e] - me
        ahead = jnp.where(ahead < -REACH, ahead + tiles, ahead)
        ahead = jnp.where(ahead > REACH, ahead - tiles, ahead)
        alive = e < count
        keys.append(jnp.where(alive, jnp.where(ahead > 0, 2 * ahead, jnp.maximum(-2 * ahead - 1, 0)), -1))
        dests.append(jnp.where(alive, dep[2, e], -1))
        rank = jnp.int32(0)
        for q in range(e):
            rank = rank + jnp.where(keys[q] == keys[e], 1, 0)
        spots.append(jnp.where(alive, keys[e] * CAP + rank, SLOTS))
        tile = jnp.where(place == spots[e], dep[1, e], tile)
    ask_out[...] = tile
    ask_in[0] = tile

    pl.semaphore_wait(barrier, tiles - 1)

    def ask_copy(r):
        return pltpu.make_async_remote_copy(
            src_ref=ask_out, dst_ref=ask_in.at[r],
            send_sem=ask_send.at[r], recv_sem=ask_recv.at[r],
            device_id={"lon": peer_at(OFFSETS[r])}, device_id_type=MESH)

    def fetch_copy(r):
        at = pl.ds(r * CAP, CAP)
        return pltpu.make_async_remote_copy(
            src_ref=sendbox.at[at], dst_ref=fetched.at[at],
            send_sem=fet_send.at[r], recv_sem=fet_recv.at[r],
            device_id={"lon": peer_at(-OFFSETS[r])}, device_id_type=MESH)

    def return_copy(r):
        at = pl.ds(r * CAP, CAP)
        return pltpu.make_async_remote_copy(
            src_ref=outbox.at[at], dst_ref=returned.at[at],
            send_sem=ret_send.at[r], recv_sem=ret_recv.at[r],
            device_id={"lon": peer_at(OFFSETS[r])}, device_id_type=MESH)

    far_first = list(range(SPAN - 1, 0, -1))
    for r in far_first:
        ask_copy(r).start()

    for e in range(entries):
        prev = jnp.int32(0)
        last = dests[e]
        for q in range(entries):
            if q != e:
                same = dests[q] == dests[e]
                prev = jnp.maximum(prev, jnp.where(same & (spots[q] < spots[e]), spots[q] + 1, 0))
                last = jnp.where(same & (spots[q] > spots[e]), -1, last)
        spot_s[e] = spots[e]
        prev_s[e] = prev
        slot_entry = jnp.where(lane == spots[e], e, slot_entry)
        special = jnp.where(lane == last, e + 1, special)
    spec_v[0] = special
    spec_v[1] = slot_entry
    spec_copy = pltpu.make_async_copy(spec_v, spec_s, small_sem.at[0])
    spec_copy.start()

    def network(y32, ct, marks):
        n = len(marks)
        y_b = y32.astype(BF16)
        pre = mm(y_b, w_in[...]) + b_in[...]
        hidden = jnp.tanh(pre)
        h_b = hidden.astype(BF16)
        ghid = mm_nt(ct, w_out[...])
        gpre = ghid * (1.0 - hidden * hidden)
        gpre_b = gpre.astype(BF16)
        ct32 = ct.astype(F32)
        out = (ct32 + mm_nt(gpre_b, w_in[...])).astype(BF16)
        y_m, ct_m, total = [], [], None
        for i in range(n):
            at = slice(i * width, (i + 1) * width)
            y_m.append((y32[at] * marks[i]).astype(BF16))
            ct_m.append((ct32[at] * marks[i]).astype(BF16))
            here = jnp.sum(gpre[at].reshape(width // 8, 8, -1), axis=0) * marks[i]
            total = here if total is None else total + here
        gsum[:feat] += mm_tn(jnp.concatenate(y_m, axis=0), gpre_b)
        gsum[feat:] += mm_tn(jnp.concatenate(ct_m, axis=0), h_b)
        dbsum[...] += total
        return out.reshape(n, width, feat)

    def step(c, carry):
        for copy in load_chunk(c):
            copy.wait()
        y, marks = [], []
        for i in range(CHUNK):
            t = c * CHUNK + i
            y.append(mm(local[t], state[t]))
            marks.append(jnp.where(spec_s[0, 0, t] == 0, 1.0, 0.0).astype(F32))
        ct = cot[pl.ds(c * CHUNK, CHUNK)].reshape(CHUNK * width, feat)
        gy[pl.ds(c * CHUNK, CHUNK)] = network(jnp.concatenate(y, axis=0), ct, marks)
        return carry

    for copy in loads[2:6]:
        copy.wait()
    spec_copy.wait()
    first = min(1, nchunks)
    lax.fori_loop(0, first, step, 0)

    for r in far_first:
        ask_copy(r).wait_recv()
    asked_copy = pltpu.make_async_copy(ask_in, ask_s, small_sem.at[1])
    asked_copy.start()
    asked_copy.wait()

    asked = [ask_s[r, r, c] for r in range(SPAN) for c in range(CAP)]
    for r in far_first + [0]:
        for k in range(r * CAP, (r + 1) * CAP):
            block = state[jnp.clip(asked[k], 0, nblocks - 1)]
            if r == 0:
                fetched[k] = block
            else:
                sendbox[k] = block
        if r != 0:
            fetch_copy(r).start()

    lax.fori_loop(first, nchunks, step, 0)

    for e in range(entries):
        d = dep[2, e]
        ysp[e] = mm(local[d], state[d])
        csp[e] = cot[d]
    loads[6].wait()
    choice = lane
    lasts = []
    for k in range(SLOTS):
        last = jnp.int32(SLOTS + k)
        for q in range(k):
            last = jnp.where(asked[q] == asked[k], q, last)
        lasts.append(last)
        choice = jnp.where(lane == asked[k], nblocks + k, choice)
    choice_v[...] = choice
    choice_copy = pltpu.make_async_copy(choice_v, choice_h, small_sem.at[2])
    choice_copy.start()

    for r in range(SPAN):
        if r != 0:
            fetch_copy(r).wait_recv()
        for k in range(r * CAP, (r + 1) * CAP):
            found = spec_s[1, 0, k]
            e = jnp.minimum(found, entries - 1)
            weight = jnp.where(found < entries, 1.0, 0.0).astype(F32)
            acc[k + 1] = mm(remote[e], fetched[k]) * weight + acc[prev_s[e]]

    @pl.loop(0, entries // CHUNK)
    def _(c):
        marks, y = [], []
        for i in range(CHUNK):
            e = c * CHUNK + i
            marks.append(jnp.where(spec_s[0, 0, dep[2, e]] == e + 1, 1.0, 0.0).astype(F32))
            y.append(ysp[e] + acc[jnp.minimum(spot_s[e], SLOTS - 1) + 1])
        ct = csp[pl.ds(c * CHUNK, CHUNK)].reshape(CHUNK * width, feat)
        gy[pl.ds(nblocks + c * CHUNK, CHUNK)] = network(jnp.concatenate(y, axis=0), ct, marks)

    mine = lax.rem(me, group)
    base = me - mine
    gout[...] = gsum[...].astype(BF16).reshape(gout.shape)
    dbin[me] = jnp.sum(dbsum[...], axis=0, keepdims=True)

    def mate(i):
        return lax.rem(mine + i, group)

    def share_copy(i):
        return pltpu.make_async_remote_copy(
            src_ref=gout.at[mate(i)], dst_ref=gin.at[i],
            send_sem=rs_send.at[i], recv_sem=rs_recv.at[i],
            device_id={"lon": base + mate(i)}, device_id_type=MESH)

    def bias_copy(i):
        return pltpu.make_async_remote_copy(
            src_ref=dbin.at[me], dst_ref=dbin.at[me],
            send_sem=db_send.at[i], recv_sem=db_recv.at[i],
            device_id={"lon": peer_at(i)}, device_id_type=MESH)

    def gather_copy(i):
        return pltpu.make_async_remote_copy(
            src_ref=red, dst_ref=gall.at[mine],
            send_sem=ag_send.at[i], recv_sem=ag_recv.at[i],
            device_id={"lon": base + mate(i)}, device_id_type=MESH)

    def cross_copy(i):
        return pltpu.make_async_remote_copy(
            src_ref=xin.at[me // group], dst_ref=xin.at[me // group],
            send_sem=x_send.at[i], recv_sem=x_recv.at[i],
            device_id={"lon": peer_at(i * group)}, device_id_type=MESH)

    @pl.loop(1, group)
    def _(i):
        share_copy(i).start()

    for r in far_first + [0]:
        for k in range(r * CAP, (r + 1) * CAP):
            e = jnp.minimum(spec_s[1, 0, k], entries - 1)
            at = jnp.maximum(spec_s[0, 0, dep[2, e]] - 1, 0) + nblocks
            value = mm_tn(remote[e], gy[at]).astype(BF16)
            if r == 0:
                returned[k] = value
            else:
                outbox[k] = value
        if r != 0:
            return_copy(r).start()

    @pl.loop(1, tiles)
    def _(i):
        bias_copy(i).start()

    def adjoint(t):
        s = spec_s[0, 0, t]
        return mm_tn(local[t], gy[jnp.where(s == 0, t, nblocks + s - 1)])

    def store_chunk(c):
        at = pl.ds(c * CHUNK, CHUNK)
        return pltpu.make_async_copy(result.at[at], blocks_h.at[at], out_sem.at[c])

    @pl.loop(0, nchunks)
    def _(c):
        for i in range(CHUNK):
            t = c * CHUNK + i
            result[t] = adjoint(t).astype(BF16)
        store_chunk(c).start()

    @pl.loop(1, group)
    def _(i):
        share_copy(i).wait_recv()

    share = gsum[pl.ds(pl.multiple_of(mine * part, part), part)]
    share = lax.fori_loop(1, group, lambda i, s: s + gin[i].astype(F32), share)
    if groups > 1:
        xin[me // group] = share.astype(BF16)

        @pl.loop(1, groups)
        def _(i):
            cross_copy(i).start()

        @pl.loop(1, groups)
        def _(i):
            cross_copy(i).wait()

        share = lax.fori_loop(
            0, groups, lambda i, s: s + xin[i].astype(F32), jnp.zeros(share.shape, F32))
    red[...] = share.astype(BF16)
    gall[mine] = share.astype(BF16)

    @pl.loop(1, group)
    def _(i):
        gather_copy(i).start()

    for k in range(SLOTS):
        racc[SLOTS + k] = adjoint(jnp.clip(asked[k], 0, nblocks - 1))
    for r in range(SPAN):
        if r != 0:
            return_copy(r).wait_recv()
        for k in range(r * CAP, (r + 1) * CAP):
            total = returned[k].astype(F32) + racc[lasts[k]]
            racc[k] = total
            patch[k] = total.astype(BF16)
    ends = [pltpu.make_async_copy(patch, blocks_h.at[pl.ds(nblocks, SLOTS)], end_sem.at[0])]
    ends[0].start()

    @pl.loop(1, tiles)
    def _(i):
        bias_copy(i).wait()

    db[...] = lax.fori_loop(1, tiles, lambda i, s: s + dbin[i], dbin[0])

    @pl.loop(1, group)
    def _(i):
        gather_copy(i).wait_recv()

    whole = gall[...].astype(F32).reshape(2 * feat, -1)
    din[...] = whole[:feat]
    dout[...] = whole[feat:].T
    for n, (src, dst) in enumerate([(db, db_h), (din, din_h), (dout, dout_h)]):
        ends.append(pltpu.make_async_copy(src, dst, end_sem.at[n + 1]))
        ends[-1].start()

    @pl.loop(1, group)
    def _(i):
        share_copy(i).wait_send()
        gather_copy(i).wait_send()

    for r in far_first:
        ask_copy(r).wait_send()
        fetch_copy(r).wait_send()
        return_copy(r).wait_send()

    @pl.loop(0, nchunks)
    def _(c):
        store_chunk(c).wait()

    choice_copy.wait()
    for copy in ends:
        copy.wait()


def finish(choice_h, blocks_h, din_h, db_h, dout_h, grad_h, din_o, db_o, dout_o,
           choice, blocks, din, db, dout, load_sem, store_sem, block_sem):
    loads = [
        pltpu.make_async_copy(src, dst, load_sem.at[n])
        for n, (src, dst) in enumerate([
            (choice_h, choice), (blocks_h, blocks), (din_h, din), (db_h, db), (dout_h, dout)])
    ]
    stores = [
        pltpu.make_async_copy(src, dst, store_sem.at[n])
        for n, (src, dst) in enumerate([(din, din_o), (db, db_o), (dout, dout_o)])
    ]
    for copy in loads:
        copy.start()
    for load, store in zip(loads[2:], stores):
        load.wait()
        store.start()
    loads[0].wait()
    loads[1].wait()
    nblocks = grad_h.shape[0]

    def move(t):
        return pltpu.make_async_copy(blocks.at[choice[0, t]], grad_h.at[t], block_sem.at[t])

    @pl.loop(0, nblocks, unroll=4)
    def _(t):
        move(t).start()

    for copy in stores:
        copy.wait()

    @pl.loop(0, nblocks, unroll=4)
    def _(t):
        move(t).wait()


def body(tiles, state, cotangent, local_interp, remote_interp, departures, counts, w_in, b_in, w_out):
    nblocks, width, _ = local_interp.shape
    feat = state.shape[1]
    hid = w_in.shape[1]
    entries = remote_interp.shape[0]
    nchunks = nblocks // CHUNK
    group = min(GROUP, tiles)
    part = 2 * feat // group
    dma = pltpu.SemaphoreType.DMA
    hbm = pl.BlockSpec(memory_space=pl.ANY)
    blk = (width, feat)
    grads = (
        jax.ShapeDtypeStruct((feat, hid), F32),
        jax.ShapeDtypeStruct((1, hid), F32),
        jax.ShapeDtypeStruct((hid, feat), F32),
    )
    blocks, choice, d_in, d_b, d_out = pl.pallas_call(
        functools.partial(kernel, tiles),
        out_shape=(
            jax.ShapeDtypeStruct((nblocks + SLOTS,) + blk, BF16),
            jax.ShapeDtypeStruct((8, 128), jnp.int32),
        ) + grads,
        in_specs=[hbm] * 9,
        out_specs=(hbm,) * 5,
        scratch_shapes=[
            pltpu.VMEM((feat, hid), BF16),
            pltpu.VMEM((1, hid), F32),
            pltpu.VMEM((hid, feat), BF16),
            pltpu.VMEM((nblocks,) + blk, BF16),
            pltpu.VMEM((nblocks,) + blk, BF16),
            pltpu.VMEM((nblocks, width, width), BF16),
            pltpu.VMEM((entries, width, width), BF16),
            pltpu.VMEM((nblocks + entries,) + blk, BF16),
            pltpu.VMEM((nblocks,) + blk, BF16),
            pltpu.VMEM((SLOTS,) + blk, BF16),
            pltpu.VMEM((SLOTS,) + blk, BF16),
            pltpu.VMEM((SLOTS,) + blk, BF16),
            pltpu.VMEM((SLOTS,) + blk, BF16),
            pltpu.VMEM((SLOTS,) + blk, BF16),
            pltpu.VMEM((SLOTS + 1,) + blk, F32),
            pltpu.VMEM((2 * SLOTS,) + blk, F32),
            pltpu.VMEM((entries,) + blk, F32),
            pltpu.VMEM((entries,) + blk, BF16),
            pltpu.VMEM((2 * feat, hid), F32),
            pltpu.VMEM((8, hid), F32),
            pltpu.VMEM((group, part, hid), BF16),
            pltpu.VMEM((group, part, hid), BF16),
            pltpu.VMEM((part, hid), BF16),
            pltpu.VMEM((group, part, hid), BF16),
            pltpu.VMEM((tiles, 1, hid), F32),
            pltpu.VMEM((tiles // group, part, hid), BF16),
            pltpu.VMEM((feat, hid), F32),
            pltpu.VMEM((1, hid), F32),
            pltpu.VMEM((hid, feat), F32),
            pltpu.VMEM((8, 128), jnp.int32),
            pltpu.VMEM((SPAN, 8, 128), jnp.int32),
            pltpu.VMEM((2, 8, 128), jnp.int32),
            pltpu.VMEM((8, 128), jnp.int32),
            pltpu.SMEM(departures.shape, jnp.int32),
            pltpu.SMEM(counts.shape, jnp.int32),
            pltpu.SMEM((SPAN, 8, 128), jnp.int32),
            pltpu.SMEM((2, 8, 128), jnp.int32),
            pltpu.SMEM((entries,), jnp.int32),
            pltpu.SMEM((entries,), jnp.int32),
            dma((7,)), dma((2, nchunks)), dma((nchunks,)), dma((4,)), dma((3,)),
            dma((SPAN,)), dma((SPAN,)), dma((SPAN,)), dma((SPAN,)), dma((SPAN,)), dma((SPAN,)),
            dma((group,)), dma((group,)), dma((tiles,)), dma((tiles,)),
            dma((group,)), dma((group,)),
            dma((max(tiles // group, 2),)), dma((max(tiles // group, 2),)),
        ],
        compiler_params=pltpu.CompilerParams(
            collective_id=0, has_side_effects=True, vmem_limit_bytes=63 * 1024 * 1024
        ),
    )(
        departures, counts, w_in, b_in.reshape(1, hid), w_out,
        state.reshape(nblocks, width, feat), cotangent.reshape(nblocks, width, feat),
        local_interp, remote_interp,
    )
    grad, d_in, d_b, d_out = pl.pallas_call(
        finish,
        out_shape=(jax.ShapeDtypeStruct((nblocks,) + blk, BF16),) + grads,
        in_specs=[hbm] * 5,
        out_specs=(hbm,) * 4,
        scratch_shapes=[
            pltpu.SMEM((8, 128), jnp.int32),
            pltpu.VMEM((nblocks + SLOTS,) + blk, BF16),
            pltpu.VMEM((feat, hid), F32),
            pltpu.VMEM((1, hid), F32),
            pltpu.VMEM((hid, feat), F32),
            dma((5,)), dma((3,)), dma((nblocks,)),
        ],
        compiler_params=pltpu.CompilerParams(vmem_limit_bytes=63 * 1024 * 1024),
    )(choice, blocks, d_in, d_b, d_out)
    return grad.reshape(nblocks * width, feat), d_in, d_b.reshape(hid), d_out


def solution(mesh):
    return jax.shard_map(
        functools.partial(body, mesh.shape["lon"]),
        mesh=mesh,
        in_specs=(
            P(("members", "lon"), None),
            P(("members", "lon"), None),
            P(("members", "lon"), None, None),
            P(("members", "lon"), None, None),
            P(None, ("members", "lon")),
            P(("members", "lon")),
            P(),
            P(),
            P(),
        ),
        out_specs=(
            P(("members", "lon"), None),
            P("members", None),
            P("members"),
            P("members", None),
        ),
        check_vma=False,
    )
```

time: 49.9 us -> 43.6 us (0.87)
  local copies, waits for them, and re-layouts: 8.81 us -> 0 us
  Pallas kernels: 39.4 us -> 42.2 us
    unnamed x16 -> x0, local copies, waits for them, and re-layouts: 8.81 us -> none
    pallas_call x0 -> x1, Pallas kernels: none -> 3.68 us  [body(): pl.pallas_call(finish, out_shape=(jax.ShapeDtypeStruct((nblocks,) + blk,...]
    pallas_call x1, Pallas kernels: 39.4 us -> 38.5 us  [body(): pl.pallas_call(functools.partial(kernel, tiles), out_shape=(jax.ShapeDtyp...]
where the time goes in v2:
time: 43.6 us; the launch traced here: 43.4 us
  Pallas kernels  42.2 us (97%)
  between operations  1.29 us (3%)
    pallas_call x1, Pallas kernels, body(): pl.pallas_call(functools.partial(kernel, tiles), out_shape=(jax.ShapeDtyp...  38.5 us
    pallas_call x1, Pallas kernels, body(): pl.pallas_call(finish, out_shape=(jax.ShapeDtypeStruct((nblocks,) + blk,...  3.68 us

profile of v2, /device:TPU:0, one launch (start us, length us, event | category | flops | bytes accessed | tf_op | source)
XLA Modules:
  0.0 43.4 jit_solution(8647291794842037438)
XLA Ops:
  1.3 38.5 %shard_map.120 = (bf16[78,128,128]{2,1,0:T(8,128)(2,1)}, s32[8,128]{1,0:T(8,128)}, f32[128,256]{1,0:T(8,128)}, f32[1,256]{1,0:T(1,128)}, f32[256,128]{1,0:T(8,128)}) custom-call(s32[3,12]{1,0:T(4,128)} %dep_h.1, s32[1]{0:T(128)S(6)} %copy.13.cnt_h, bf16[128,256]{1,0:T(8,128)(2,1)} %w_in_h.1, f32[1,256]{1,0:T(1,128)} %bitcast.7, bf16[256,128]{1,0:T(8,128)(2,1)} %w_out_h.1, ...), custom_call_target="tpu_custom_call" | custom-call | tf_op jit(solution)/shard_map/pallas_call | solution.py:447
  39.8 3.7 %shard_map.121 = (bf16[64,128,128]{2,1,0:T(8,128)(2,1)}, f32[128,256]{1,0:T(8,128)}, f32[1,256]{1,0:T(1,128)}, f32[256,128]{1,0:T(8,128)}) custom-call(s32[8,128]{1,0:T(8,128)} %get-tuple-element.13.choice_h, bf16[78,128,128]{2,1,0:T(8,128)(2,1)} %get-tuple-element.14.blocks_h, f32[128,256]{1,0:T(8,128)} %get-tuple-element.15.din_h, ...), custom_call_target="tpu_custom_call" | custom-call | tf_op jit(solution)/shard_map/pallas_call | solution.py:509

commit v3 on v2

--- a/solution.py
+++ b/solution.py
@@ -13,7 +13,10 @@
 OFFSETS = [0] + [sign * d for d in range(1, REACH + 1) for sign in (-1, 1)]
 SLOTS = SPAN * CAP
 GROUP = 16
-CHUNK = 4
+CHUNK = 8
+LIST_STEPS = 1
+MARKS = (0, 2, 2, 6)
+PIECES = 4
 MESH = pl.DeviceIdType.MESH
 F32 = jnp.float32
 BF16 = jnp.bfloat16
@@ -113,32 +116,6 @@
     ask_out[...] = tile
     ask_in[0] = tile
 
-    pl.semaphore_wait(barrier, tiles - 1)
-
-    def ask_copy(r):
-        return pltpu.make_async_remote_copy(
-            src_ref=ask_out, dst_ref=ask_in.at[r],
-            send_sem=ask_send.at[r], recv_sem=ask_recv.at[r],
-            device_id={"lon": peer_at(OFFSETS[r])}, device_id_type=MESH)
-
-    def fetch_copy(r):
-        at = pl.ds(r * CAP, CAP)
-        return pltpu.make_async_remote_copy(
-            src_ref=sendbox.at[at], dst_ref=fetched.at[at],
-            send_sem=fet_send.at[r], recv_sem=fet_recv.at[r],
-            device_id={"lon": peer_at(-OFFSETS[r])}, device_id_type=MESH)
-
-    def return_copy(r):
-        at = pl.ds(r * CAP, CAP)
-        return pltpu.make_async_remote_copy(
-            src_ref=outbox.at[at], dst_ref=returned.at[at],
-            send_sem=ret_send.at[r], recv_sem=ret_recv.at[r],
-            device_id={"lon": peer_at(OFFSETS[r])}, device_id_type=MESH)
-
-    far_first = list(range(SPAN - 1, 0, -1))
-    for r in far_first:
-        ask_copy(r).start()
-
     for e in range(entries):
         prev = jnp.int32(0)
         last = dests[e]
@@ -179,9 +156,13 @@
         dbsum[...] += total
         return out.reshape(n, width, feat)
 
-    def step(c, carry):
+    def arrive(c):
         for copy in load_chunk(c):
             copy.wait()
+
+    def step(c, carry, wait=True):
+        if wait:
+            arrive(c)
         y, marks = [], []
         for i in range(CHUNK):
             t = c * CHUNK + i
@@ -191,16 +172,44 @@
         gy[pl.ds(c * CHUNK, CHUNK)] = network(jnp.concatenate(y, axis=0), ct, marks)
         return carry
 
+    reach = [min(n, nchunks) for n in MARKS]
     for copy in loads[2:6]:
         copy.wait()
     spec_copy.wait()
-    first = min(1, nchunks)
-    lax.fori_loop(0, first, step, 0)
-
+    lax.fori_loop(0, reach[0], step, 0)
+
+    pl.semaphore_wait(barrier, tiles - 1)
+
+    def ask_copy(r):
+        return pltpu.make_async_remote_copy(
+            src_ref=ask_out, dst_ref=ask_in.at[r],
+            send_sem=ask_send.at[r], recv_sem=ask_recv.at[r],
+            device_id={"lon": peer_at(OFFSETS[r])}, device_id_type=MESH)
+
+    def fetch_copy(r):
+        at = pl.ds(r * CAP, CAP)
+        return pltpu.make_async_remote_copy(
+            src_ref=sendbox.at[at], dst_ref=fetched.at[at],
+            send_sem=fet_send.at[r], recv_sem=fet_recv.at[r],
+            device_id={"lon": peer_at(-OFFSETS[r])}, device_id_type=MESH)
+
+    def return_copy(r):
+        at = pl.ds(r * CAP, CAP)
+        return pltpu.make_async_remote_copy(
+            src_ref=outbox.at[at], dst_ref=returned.at[at],
+            send_sem=ret_send.at[r], recv_sem=ret_recv.at[r],
+            device_id={"lon": peer_at(OFFSETS[r])}, device_id_type=MESH)
+
+    far_first = list(range(SPAN - 1, 0, -1))
+    for r in far_first:
+        ask_copy(r).start()
+
+    lax.fori_loop(reach[0], reach[1], step, 0)
     for r in far_first:
         ask_copy(r).wait_recv()
     asked_copy = pltpu.make_async_copy(ask_in, ask_s, small_sem.at[1])
     asked_copy.start()
+    lax.fori_loop(reach[1], reach[2], step, 0)
     asked_copy.wait()
 
     asked = [ask_s[r, r, c] for r in range(SPAN) for c in range(CAP)]
@@ -214,7 +223,12 @@
         if r != 0:
             fetch_copy(r).start()
 
-    lax.fori_loop(first, nchunks, step, 0)
+    early = reach[3]
+    lax.fori_loop(reach[2], early, step, 0)
+
+    @pl.loop(early, nchunks)
+    def _(c):
+        arrive(c)
 
     for e in range(entries):
         d = dep[2, e]
@@ -242,51 +256,17 @@
             weight = jnp.where(found < entries, 1.0, 0.0).astype(F32)
             acc[k + 1] = mm(remote[e], fetched[k]) * weight + acc[prev_s[e]]
 
-    @pl.loop(0, entries // CHUNK)
+    few = entries // LIST_STEPS
+
+    @pl.loop(0, LIST_STEPS)
     def _(c):
         marks, y = [], []
-        for i in range(CHUNK):
-            e = c * CHUNK + i
+        for i in range(few):
+            e = c * few + i
             marks.append(jnp.where(spec_s[0, 0, dep[2, e]] == e + 1, 1.0, 0.0).astype(F32))
             y.append(ysp[e] + acc[jnp.minimum(spot_s[e], SLOTS - 1) + 1])
-        ct = csp[pl.ds(c * CHUNK, CHUNK)].reshape(CHUNK * width, feat)
-        gy[pl.ds(nblocks + c * CHUNK, CHUNK)] = network(jnp.concatenate(y, axis=0), ct, marks)
-
-    mine = lax.rem(me, group)
-    base = me - mine
-    gout[...] = gsum[...].astype(BF16).reshape(gout.shape)
-    dbin[me] = jnp.sum(dbsum[...], axis=0, keepdims=True)
-
-    def mate(i):
-        return lax.rem(mine + i, group)
-
-    def share_copy(i):
-        return pltpu.make_async_remote_copy(
-            src_ref=gout.at[mate(i)], dst_ref=gin.at[i],
-            send_sem=rs_send.at[i], recv_sem=rs_recv.at[i],
-            device_id={"lon": base + mate(i)}, device_id_type=MESH)
-
-    def bias_copy(i):
-        return pltpu.make_async_remote_copy(
-            src_ref=dbin.at[me], dst_ref=dbin.at[me],
-            send_sem=db_send.at[i], recv_sem=db_recv.at[i],
-            device_id={"lon": peer_at(i)}, device_id_type=MESH)
-
-    def gather_copy(i):
-        return pltpu.make_async_remote_copy(
-            src_ref=red, dst_ref=gall.at[mine],
-            send_sem=ag_send.at[i], recv_sem=ag_recv.at[i],
-            device_id={"lon": base + mate(i)}, device_id_type=MESH)
-
-    def cross_copy(i):
-        return pltpu.make_async_remote_copy(
-            src_ref=xin.at[me // group], dst_ref=xin.at[me // group],
-            send_sem=x_send.at[i], recv_sem=x_recv.at[i],
-            device_id={"lon": peer_at(i * group)}, device_id_type=MESH)
-
-    @pl.loop(1, group)
-    def _(i):
-        share_copy(i).start()
+        ct = csp[pl.ds(c * few, few)].reshape(few * width, feat)
+        gy[pl.ds(nblocks + c * few, few)] = network(jnp.concatenate(y, axis=0), ct, marks)
 
     for r in far_first + [0]:
         for k in range(r * CAP, (r + 1) * CAP):
@@ -300,6 +280,44 @@
         if r != 0:
             return_copy(r).start()
 
+    lax.fori_loop(early, nchunks, functools.partial(step, wait=False), 0)
+
+    mine = lax.rem(me, group)
+    base = me - mine
+    gout[...] = gsum[...].astype(BF16).reshape(gout.shape)
+    dbin[me] = jnp.sum(dbsum[...], axis=0, keepdims=True)
+
+    def mate(i):
+        return lax.rem(mine + i, group)
+
+    def share_copy(i):
+        return pltpu.make_async_remote_copy(
+            src_ref=gout.at[mate(i)], dst_ref=gin.at[i],
+            send_sem=rs_send.at[i], recv_sem=rs_recv.at[i],
+            device_id={"lon": base + mate(i)}, device_id_type=MESH)
+
+    def bias_copy(i):
+        return pltpu.make_async_remote_copy(
+            src_ref=dbin.at[me], dst_ref=dbin.at[me],
+            send_sem=db_send.at[i], recv_sem=db_recv.at[i],
+            device_id={"lon": peer_at(i)}, device_id_type=MESH)
+
+    def gather_copy(i):
+        return pltpu.make_async_remote_copy(
+            src_ref=red, dst_ref=gall.at[mine],
+            send_sem=ag_send.at[i], recv_sem=ag_recv.at[i],
+            device_id={"lon": base + mate(i)}, device_id_type=MESH)
+
+    def cross_copy(i):
+        return pltpu.make_async_remote_copy(
+            src_ref=xin.at[me // group], dst_ref=xin.at[me // group],
+            send_sem=x_send.at[i], recv_sem=x_recv.at[i],
+            device_id={"lon": peer_at(i * group)}, device_id_type=MESH)
+
+    @pl.loop(1, group)
+    def _(i):
+        share_copy(i).start()
+
     @pl.loop(1, tiles)
     def _(i):
         bias_copy(i).start()
@@ -394,32 +412,46 @@
 
 
 def finish(choice_h, blocks_h, din_h, db_h, dout_h, grad_h, din_o, db_o, dout_o,
-           choice, blocks, din, db, dout, load_sem, store_sem, block_sem):
+           choice, blocks, din, db, dout, load_sem, store_sem, part_sem, block_sem):
+    nblocks = grad_h.shape[0]
+    patches = pl.ds(nblocks, SLOTS)
     loads = [
         pltpu.make_async_copy(src, dst, load_sem.at[n])
         for n, (src, dst) in enumerate([
-            (choice_h, choice), (blocks_h, blocks), (din_h, din), (db_h, db), (dout_h, dout)])
+            (choice_h, choice), (blocks_h.at[patches], blocks.at[patches]),
+            (din_h, din), (db_h, db), (dout_h, dout)])
     ]
     stores = [
         pltpu.make_async_copy(src, dst, store_sem.at[n])
         for n, (src, dst) in enumerate([(din, din_o), (db, db_o), (dout, dout_o)])
     ]
-    for copy in loads:
+    piece = nblocks // PIECES
+
+    def load_piece(p):
+        at = pl.ds(p * piece, piece)
+        return pltpu.make_async_copy(blocks_h.at[at], blocks.at[at], part_sem.at[p])
+
+    def move(t):
+        return pltpu.make_async_copy(blocks.at[choice[0, t]], grad_h.at[t], block_sem.at[t])
+
+    for copy in loads[:2]:
         copy.start()
+    for p in range(PIECES):
+        load_piece(p).start()
+    for copy in loads[2:]:
+        copy.start()
+    for copy in loads[:2]:
+        copy.wait()
+    for p in range(PIECES):
+        load_piece(p).wait()
+
+        @pl.loop(p * piece, (p + 1) * piece, unroll=4)
+        def _(t):
+            move(t).start()
+
     for load, store in zip(loads[2:], stores):
         load.wait()
         store.start()
-    loads[0].wait()
-    loads[1].wait()
-    nblocks = grad_h.shape[0]
-
-    def move(t):
-        return pltpu.make_async_copy(blocks.at[choice[0, t]], grad_h.at[t], block_sem.at[t])
-
-    @pl.loop(0, nblocks, unroll=4)
-    def _(t):
-        move(t).start()
-
     for copy in stores:
         copy.wait()
 
@@ -517,7 +549,7 @@
             pltpu.VMEM((feat, hid), F32),
             pltpu.VMEM((1, hid), F32),
             pltpu.VMEM((hid, feat), F32),
-            dma((5,)), dma((3,)), dma((nblocks,)),
+            dma((5,)), dma((3,)), dma((PIECES,)), dma((nblocks,)),
         ],
         compiler_params=pltpu.CompilerParams(vmem_limit_bytes=63 * 1024 * 1024),
     )(choice, blocks, d_in, d_b, d_out)

time: 43.6 us -> 41 us (0.940)
  Pallas kernels: 42.2 us -> 39.5 us
    pallas_call x1, Pallas kernels: 38.5 us -> 36.1 us  [body(): pl.pallas_call(functools.partial(kernel, tiles), out_shape=(jax.ShapeDtyp...]
where the time goes in v3:
time: 41 us; the launch traced here: 40.8 us
  Pallas kernels  39.5 us (96%)
  between operations  1.29 us (3%)
    pallas_call x1, Pallas kernels, body(): pl.pallas_call(functools.partial(kernel, tiles), out_shape=(jax.ShapeDtyp...  36.1 us
    pallas_call x1, Pallas kernels, body(): pl.pallas_call(finish, out_shape=(jax.ShapeDtypeStruct((nblocks,) + blk,...  3.39 us

profile of v3, /device:TPU:0, one launch (start us, length us, event | category | flops | bytes accessed | tf_op | source)
XLA Modules:
  0.0 40.8 jit_solution(9333156674500670254)
XLA Ops:
  1.3 36.1 %shard_map.120 = (bf16[78,128,128]{2,1,0:T(8,128)(2,1)}, s32[8,128]{1,0:T(8,128)}, f32[128,256]{1,0:T(8,128)}, f32[1,256]{1,0:T(1,128)}, f32[256,128]{1,0:T(8,128)}) custom-call(s32[3,12]{1,0:T(4,128)} %dep_h.1, s32[1]{0:T(128)S(6)} %copy.13.cnt_h, bf16[128,256]{1,0:T(8,128)(2,1)} %w_in_h.1, f32[1,256]{1,0:T(1,128)} %bitcast.7, bf16[256,128]{1,0:T(8,128)(2,1)} %w_out_h.1, ...), custom_call_target="tpu_custom_call" | custom-call | tf_op jit(solution)/shard_map/pallas_call | solution.py:479
  37.4 3.4 %shard_map.121 = (bf16[64,128,128]{2,1,0:T(8,128)(2,1)}, f32[128,256]{1,0:T(8,128)}, f32[1,256]{1,0:T(1,128)}, f32[256,128]{1,0:T(8,128)}) custom-call(s32[8,128]{1,0:T(8,128)} %get-tuple-element.13.choice_h, bf16[78,128,128]{2,1,0:T(8,128)(2,1)} %get-tuple-element.14.blocks_h, f32[128,256]{1,0:T(8,128)} %get-tuple-element.15.din_h, ...), custom_call_target="tpu_custom_call" | custom-call | tf_op jit(solution)/shard_map/pallas_call | solution.py:541

commit v4 on v3

--- a/solution.py
+++ b/solution.py
@@ -15,7 +15,7 @@
 GROUP = 16
 CHUNK = 8
 LIST_STEPS = 1
-MARKS = (0, 2, 2, 6)
+MARKS = (0, 2, 2, 7)
 PIECES = 4
 MESH = pl.DeviceIdType.MESH
 F32 = jnp.float32
@@ -268,6 +268,44 @@
         ct = csp[pl.ds(c * few, few)].reshape(few * width, feat)
         gy[pl.ds(nblocks + c * few, few)] = network(jnp.concatenate(y, axis=0), ct, marks)
 
+    lax.fori_loop(early, nchunks, functools.partial(step, wait=False), 0)
+
+    mine = lax.rem(me, group)
+    base = me - mine
+    gout[...] = gsum[...].astype(BF16).reshape(gout.shape)
+    dbin[me] = jnp.sum(dbsum[...], axis=0, keepdims=True)
+
+    def mate(i):
+        return lax.rem(mine + i, group)
+
+    def share_copy(i):
+        return pltpu.make_async_remote_copy(
+            src_ref=gout.at[mate(i)], dst_ref=gin.at[i],
+            send_sem=rs_send.at[i], recv_sem=rs_recv.at[i],
+            device_id={"lon": base + mate(i)}, device_id_type=MESH)
+
+    def bias_copy(i):
+        return pltpu.make_async_remote_copy(
+            src_ref=dbin.at[me], dst_ref=dbin.at[me],
+            send_sem=db_send.at[i], recv_sem=db_recv.at[i],
+            device_id={"lon": peer_at(i)}, device_id_type=MESH)
+
+    def gather_copy(i):
+        return pltpu.make_async_remote_copy(
+            src_ref=red, dst_ref=gall.at[mine],
+            send_sem=ag_send.at[i], recv_sem=ag_recv.at[i],
+            device_id={"lon": base + mate(i)}, device_id_type=MESH)
+
+    def cross_copy(i):
+        return pltpu.make_async_remote_copy(
+            src_ref=xin.at[me // group], dst_ref=xin.at[me // group],
+            send_sem=x_send.at[i], recv_sem=x_recv.at[i],
+            device_id={"lon": peer_at(i * group)}, device_id_type=MESH)
+
+    @pl.loop(1, group)
+    def _(i):
+        share_copy(i).start()
+
     for r in far_first + [0]:
         for k in range(r * CAP, (r + 1) * CAP):
             e = jnp.minimum(spec_s[1, 0, k], entries - 1)
@@ -279,44 +317,6 @@
                 outbox[k] = value
         if r != 0:
             return_copy(r).start()
-
-    lax.fori_loop(early, nchunks, functools.partial(step, wait=False), 0)
-
-    mine = lax.rem(me, group)
-    base = me - mine
-    gout[...] = gsum[...].astype(BF16).reshape(gout.shape)
-    dbin[me] = jnp.sum(dbsum[...], axis=0, keepdims=True)
-
-    def mate(i):
-        return lax.rem(mine + i, group)
-
-    def share_copy(i):
-        return pltpu.make_async_remote_copy(
-            src_ref=gout.at[mate(i)], dst_ref=gin.at[i],
-            send_sem=rs_send.at[i], recv_sem=rs_recv.at[i],
-            device_id={"lon": base + mate(i)}, device_id_type=MESH)
-
-    def bias_copy(i):
-        return pltpu.make_async_remote_copy(
-            src_ref=dbin.at[me], dst_ref=dbin.at[me],
-            send_sem=db_send.at[i], recv_sem=db_recv.at[i],
-            device_id={"lon": peer_at(i)}, device_id_type=MESH)
-
-    def gather_copy(i):
-        return pltpu.make_async_remote_copy(
-            src_ref=red, dst_ref=gall.at[mine],
-            send_sem=ag_send.at[i], recv_sem=ag_recv.at[i],
-            device_id={"lon": base + mate(i)}, device_id_type=MESH)
-
-    def cross_copy(i):
-        return pltpu.make_async_remote_copy(
-            src_ref=xin.at[me // group], dst_ref=xin.at[me // group],
-            send_sem=x_send.at[i], recv_sem=x_recv.at[i],
-            device_id={"lon": peer_at(i * group)}, device_id_type=MESH)
-
-    @pl.loop(1, group)
-    def _(i):
-        share_copy(i).start()
 
     @pl.loop(1, tiles)
     def _(i):

time: 41 us -> 38.7 us (0.944)
  Pallas kernels: 39.5 us -> 37.1 us
    pallas_call x1, Pallas kernels: 36.1 us -> 33.8 us  [body(): pl.pallas_call(functools.partial(kernel, tiles), out_shape=(jax.ShapeDtyp...]
where the time goes in v4:
time: 38.7 us; the launch traced here: 38.4 us
  Pallas kernels  37.1 us (96%)
  between operations  1.29 us (3%)
    pallas_call x1, Pallas kernels, body(): pl.pallas_call(functools.partial(kernel, tiles), out_shape=(jax.ShapeDtyp...  33.8 us
    pallas_call x1, Pallas kernels, body(): pl.pallas_call(finish, out_shape=(jax.ShapeDtypeStruct((nblocks,) + blk,...  3.39 us

profile of v4, /device:TPU:0, one launch (start us, length us, event | category | flops | bytes accessed | tf_op | source)
XLA Modules:
  0.0 38.4 jit_solution(8050219136428697340)
XLA Ops:
  1.3 33.8 %shard_map.120 = (bf16[78,128,128]{2,1,0:T(8,128)(2,1)}, s32[8,128]{1,0:T(8,128)}, f32[128,256]{1,0:T(8,128)}, f32[1,256]{1,0:T(1,128)}, f32[256,128]{1,0:T(8,128)}) custom-call(s32[3,12]{1,0:T(4,128)} %dep_h.1, s32[1]{0:T(128)S(6)} %copy.13.cnt_h, bf16[128,256]{1,0:T(8,128)(2,1)} %w_in_h.1, f32[1,256]{1,0:T(1,128)} %bitcast.7, bf16[256,128]{1,0:T(8,128)(2,1)} %w_out_h.1, ...), custom_call_target="tpu_custom_call" | custom-call | tf_op jit(solution)/shard_map/pallas_call | solution.py:479
  35.0 3.4 %shard_map.121 = (bf16[64,128,128]{2,1,0:T(8,128)(2,1)}, f32[128,256]{1,0:T(8,128)}, f32[1,256]{1,0:T(1,128)}, f32[256,128]{1,0:T(8,128)}) custom-call(s32[8,128]{1,0:T(8,128)} %get-tuple-element.13.choice_h, bf16[78,128,128]{2,1,0:T(8,128)(2,1)} %get-tuple-element.14.blocks_h, f32[128,256]{1,0:T(8,128)} %get-tuple-element.15.din_h, ...), custom_call_target="tpu_custom_call" | custom-call | tf_op jit(solution)/shard_map/pallas_call | solution.py:541
